TPU v7x, 32 devices: a whole 2x2x4 slice. The times are simulated.
32 devices in a mesh: dp: 8 (over z, y), seq: 4 (over x, core).
Axes of the slice: x: 2, y: 2, z: 4, core: 2. Of those that a mesh axis runs over, the one named last changes fastest.
Arguments:
- bases: int32 [8, 6144], P('dp', 'seq'), may hold values from 0 to 3
- embed_weight: bfloat16 [15, 4, 768], P(None, None, 'dp'), may hold values from -1.5 to 1.5
- embed_bias: bfloat16 [768], P('dp'), may hold values from -3 to 3
- norm_gain: bfloat16 [768], P('dp'), may hold values from 0.5 to 1.5
- proj_weight: bfloat16 [768, 896], P('dp'), may hold values from -0.21875 to 0.21875
- proj_bias: bfloat16 [896], P('dp'), may hold values from -3 to 3
- cotangent: bfloat16 [8, 3072, 896], P('dp', 'seq'), may hold values from -6 to 6
Outputs:
- pooled: bfloat16 [8, 3072, 896], P('dp', 'seq')
- grad_embed_weight: float32 [15, 4, 768], P(None, None, 'dp')
- grad_embed_bias: float32 [768], P('dp')
- grad_norm_gain: float32 [768], P('dp')
- grad_proj_weight: float32 [768, 896], P('dp')
- grad_proj_bias: float32 [896], P('dp')
All inputs are finite; a program needn't handle non-finite values.
Results may differ from a plain program's by a relative error of at most 0.0065.
Values may be sent and summed in bfloat16 or wider, within the bound.
A program may use at most 64 MiB of HBM per device.

v0:
```python
import jax
import jax.numpy as jnp
from jax import lax
from jax.sharding import PartitionSpec as P


def with_halo(x, sides, width):
    for axis, dim in sides:
        devices, length = (lax.axis_size(axis), x.shape[dim])
        up = [(i, (i + 1) % devices) for i in range(devices - 1)]
        down = [(j, i) for i, j in up]
        last = lax.slice_in_dim(x, length - width, length, axis=dim)
        leading = lax.slice_in_dim(x, 0, width, axis=dim)
        before = lax.ppermute(last, axis, up)
        after = lax.ppermute(leading, axis, down)
        x = jnp.concatenate([before, x, after], axis=dim)
    return x


def local(bases, embed_weight, embed_bias, norm_gain, proj_weight, proj_bias, cotangent):
    kernel_width = embed_weight.shape[0]
    row_count = bases.shape[1]
    codes = bases + 1
    padded = with_halo(codes, (("seq", 1),), kernel_width // 2)[0]
    full_embed, full_bias, full_gain, full_proj, full_proj_bias = (
        lax.all_gather(embed_weight, "dp", axis=2, tiled=True),
        lax.all_gather(embed_bias, "dp", axis=0, tiled=True),
        lax.all_gather(norm_gain, "dp", axis=0, tiled=True),
        lax.all_gather(proj_weight, "dp", axis=0, tiled=True),
        lax.all_gather(proj_bias, "dp", axis=0, tiled=True),
    )
    letters = jnp.arange(1, 5, dtype=jnp.int32)
    features = jnp.concatenate(
        [
            (padded[k : k + row_count, None] == letters).astype(jnp.bfloat16)
            for k in range(kernel_width)
        ],
        axis=1,
    )
    flat_weight = full_embed.reshape(kernel_width * 4, -1)
    embedded = (
        jnp.dot(features, flat_weight, preferred_element_type=jnp.float32)
        + full_bias.astype(jnp.float32)
    ).astype(jnp.bfloat16)
    values = embedded.astype(jnp.float32)
    inverse = lax.rsqrt(jnp.mean(values * values, axis=1, keepdims=True) + 1e-06)
    scaled = values * inverse
    normed = scaled * full_gain.astype(jnp.float32)
    activated = jax.nn.gelu(normed, approximate=True).astype(jnp.bfloat16)
    product = jnp.dot(activated, full_proj, preferred_element_type=jnp.float32)
    mixed = product + full_proj_bias.astype(jnp.float32)
    pooled = jnp.mean(mixed.reshape(row_count // 2, 2, -1), axis=1).astype(jnp.bfloat16)
    scale_factor = 0.5 / (row_count * lax.axis_size("seq") * lax.axis_size("dp"))
    grad_mixed = (jnp.repeat(cotangent[0].astype(jnp.float32), 2, axis=0) * scale_factor).astype(
        jnp.bfloat16
    )
    grad_proj_weight = lax.dot_general(
        activated, grad_mixed, (((0,), (0,)), ((), ())), preferred_element_type=jnp.float32
    )
    grad_proj_bias = jnp.sum(grad_mixed.astype(jnp.float32), axis=0)
    grad_activated = lax.dot_general(
        grad_mixed, full_proj, (((1,), (1,)), ((), ())), preferred_element_type=jnp.float32
    )
    _, pullback = jax.vjp(lambda v: jax.nn.gelu(v, approximate=True), normed)
    grad_normed = pullback(grad_activated)[0]
    grad_norm_gain = jnp.sum(grad_normed * scaled, axis=0)
    weighted = grad_normed * full_gain.astype(jnp.float32)
    grad_embedded = (
        inverse * (weighted - scaled * jnp.mean(weighted * scaled, axis=1, keepdims=True))
    ).astype(jnp.bfloat16)
    grad_embed_weight = lax.dot_general(
        features, grad_embedded, (((0,), (0,)), ((), ())), preferred_element_type=jnp.float32
    ).reshape(kernel_width, 4, -1)
    grad_embed_bias = jnp.sum(grad_embedded.astype(jnp.float32), axis=0)
    whole = lax.psum(
        (grad_embed_weight, grad_embed_bias, grad_norm_gain, grad_proj_weight, grad_proj_bias),
        "seq",
    )
    results = (
        lax.psum_scatter(whole[0], "dp", scatter_dimension=2, tiled=True),
        lax.psum_scatter(whole[1], "dp", scatter_dimension=0, tiled=True),
        lax.psum_scatter(whole[2], "dp", scatter_dimension=0, tiled=True),
        lax.psum_scatter(whole[3], "dp", scatter_dimension=0, tiled=True),
        lax.psum_scatter(whole[4], "dp", scatter_dimension=0, tiled=True),
    )
    return (pooled[None], results[0], results[1], results[2], results[3], results[4])


def solution(mesh):
    placed = (
        P("dp", "seq"),
        P(None, None, "dp"),
        P("dp"),
        P("dp"),
        P("dp", None),
        P("dp"),
        P("dp", "seq", None),
    )
    return jax.shard_map(
        local,
        mesh=mesh,
        in_specs=placed,
        out_specs=(
            P("dp", "seq", None),
            P(None, None, "dp"),
            P("dp"),
            P("dp"),
            P("dp", None),
            P("dp"),
        ),
        check_vma=False,
    )
```

profile of v0, /device:TPU:0, one launch (start us, length us, event | category | flops | bytes accessed | tf_op | source)
XLA Modules:
  0.0 290.8 jit_solution(126104127223599485)
XLA Ops:
  9.3 1.3 collective-permute-start.1
  10.6 3.6 %collective-permute-start = (s32[1,7]{1,0:T(1,128)}, s32[1,7]{1,0:T(1,128)}, u32[]{:S(2)}, u32[]{:S(2)}) collective-permute-start(s32[1,7]{1,0:T(1,128)} %get-tuple-element.40), channel_id=1, source_target_pairs={{0,1},{1,2},{2,3},{4,5},{5,6},{6,7},{8,9},{9,10},{10,11},{12,13},{... | collective-permute-start | bytes 92 | tf_op jit(solution)/shard_map/ppermute | solution.py:14
  14.2 1.3 fusion.57
  16.8 2.7 fusion.50
  20.2 24.2 %all-reduce.8 = (bf16[896]{0:T(1024)(128)(2,1)}, bf16[768]{0:T(1024)(128)(2,1)S(1)}, bf16[768]{0:T(1024)(128)(2,1)S(1)}) all-reduce(bf16[896]{0:T(1024)(128)(2,1)S(1)} %dynamic-update-slice.2, bf16[768]{0:T(1024)(128)(2,1)S(1)} %dynamic-update-slice, bf16[768]{0:T(1024)(128)(2,1)S(1)} %dynamic-update-slice.1), channel_id=1, replica_groups=mesh['dp'=8,'seq'=4] {'dp'}, use_global_device_ids=true, to_apply=%add.2 | all-reduce | flops 2432 | bytes 9728
  46.4 32.4 %all_gather.15 = bf16[15,4,768]{0,1,2:T(4,128)(2,1)S(1)} all-gather(bf16[15,4,96]{0,1,2:T(4,128)(2,1)} %copy.16), channel_id=1, replica_groups=mesh['dp'=8,'seq'=4] {'dp'}, dimensions={2}, use_global_device_ids=true | all-gather | bytes 103680 | tf_op jit(solution)/shard_map/all_gather | solution.py:26
  78.8 1.1 copy.17
  79.9 1.6 reshape.111
  81.5 4.3 %broadcast_in_dim.4 = bf16[768,2,896]{2,1,0:T(2,128)(2,1)} broadcast(bf16[768,896]{1,0:T(8,128)(2,1)} %get-tuple-element.36), dimensions={0,2} | broadcast | bytes 4128768 | tf_op jit(solution)/shard_map/broadcast_in_dim | solution.py:54
  85.8 6.8 %convert_element_type.87 = bf16[1536,896]{1,0:T(8,128)(2,1)} reshape(bf16[768,2,896]{2,1,0:T(2,128)(2,1)} %broadcast_in_dim.4) | data formatting | bytes 5505024 | tf_op jit(solution)/shard_map/convert_element_type | solution.py:54
  93.4 1.1 fusion.36
  94.4 1.0 fusion.35
  95.4 5.0 %broadcast_compare_fusion = (pred[1536,4]{1,0:T(32,128)(4,1)S(1)}, pred[1536,4]{1,0:T(32,128)(4,1)S(1)}, pred[1536,4]{1,0:T(32,128)(4,1)S(1)}, pred[1536,4]{1,0:...) fusion(s32[4]{0:T(128)S(1)} %iota_add_fusion, ...), kind=kLoop, calls=%fused_computation.33 | loop fusion | flops 92160 | bytes 184336 | tf_op jit(solution)/shard_map/eq | solution.py:35
  100.4 6.3 %concatenate.27 = pred[1536,60]{1,0:T(32,128)(4,1)} concatenate(pred[1536,4]{1,0:T(32,128)(4,1)} %get-tuple-element.57, pred[1536,4]{1,0:T(32,128)(4,1)S(1)} %get-tuple-element.44, pred[1536,4]{1,0:T(32,128)(4,1)S(1)} %get-tuple-element.45, pred[1536,4]{1,0:T(32,128)(4,1)S(1)} %get-tuple-element.46, pred[1536,4]{1,0:T(32,128)(4,1)} %get-tuple-element.47, ...), dimensions={1} | concatenate | bytes 184320 | tf_op jit(solution)/shard_map/concatenate | solution.py:33
  106.8 1.8 fusion.17
  108.6 1.4 copy-done
  110.0 6.7 %fusion.51 = f32[768,896]{1,0:T(8,128)} fusion(bf16[1536,896]{1,0:T(8,128)(2,1)} %convert_element_type.87, bf16[1536,768]{1,0:T(8,128)(2,1)S(1)} %get-tuple-element.59, f32[768]{0:T(1024)S(1)} %copy-done.3, f32[1536]{0:T(1024)S(1)} %add_rsqrt_fusion), kind=kOutput, calls=%fused_computation.94 | convolution fusion | flops 2128084992 | bytes 7873536 | tf_op jit(solution)/shard_map/dot_general | solution.py:57
  118.6 8.4 %fusion.16 = (f32[768]{0:T(1024)S(1)}, f32[1536]{0:T(1024)S(1)}, f32[1536,768]{1,0:T(8,128)S(1)}) fusion(bf16[1536,768]{1,0:T(8,128)(2,1)} %copy-done, f32[1536]{0:T(1024)S(1)} %add_rsqrt_fusion, f32[768]{0:T(1024)S(1)} %copy-done.3, bf16[1536,896]{1,0:T(8,128)(2,1)} %convert_element_type.87, bf16[768,896]{1,0:T(8,128)(2,1)} %all-gather.2.cloned.1.call-done), kind=kOutput, calls=%fused_computation.20 | convolution fusion | flops 2145777408 | bytes 11225088 | tf_op jit(solution)/shard_map/dot_general | solution.py:61
  127.1 1.5 convert_reduce_fusion
  129.2 4.8 %copy.18 = f32[15,4,768]{1,0,2:T(8,128)} copy(f32[15,4,768]{2,1,0:T(4,128)S(1)} %reshape.113) | data formatting | bytes 368640
  134.1 5.8 %reshape.129 = f32[768,60]{1,0:T(8,128)} reshape(f32[768,15,4]{2,1,0:T(8,128)} %bitcast.19) | data formatting | bytes 368640
  140.2 6.7 %convolution_add_fusion = f32[1536,896]{1,0:T(8,128)} fusion(bf16[768,896]{1,0:T(8,128)(2,1)} %all-gather.2.cloned.1.call-done, f32[896]{0:T(1024)S(1)} %convert_element_type.81, bf16[1536,768]{1,0:T(8,128)(2,1)S(1)} %copy-done.1, f32[768]{0:T(1024)S(1)} %copy-done.3, f32[1536]{0:T(1024)S(1)} %add_rsqrt_fusion), kind=kOutput, calls=%fused_computation.27 | convolution fusion | flops 2129461248 | bytes 9253376 | tf_op jit(solution)/shard_map/dot_general | solution.py:50
  146.9 7.6 %reshape.112 = f32[768,2,896]{2,1,0:T(2,128)} reshape(f32[1536,896]{1,0:T(8,128)} %convolution_add_fusion) | data formatting | bytes 11010048 | tf_op jit(solution)/shard_map/reshape | solution.py:52
  154.5 9.2 %reduce_sum.55 = f32[768,896]{1,0:T(8,128)S(1)} reduce(f32[768,2,896]{2,1,0:T(2,128)} %reshape.112, f32[]{:T(128)} %constant.4.clone.1), dimensions={1}, to_apply=%region_1.0 | reduce | flops 688128 | bytes 8257540 | tf_op jit(solution)/shard_map/reduce_sum | solution.py:52
  163.7 21.7 %reduce-scatter.5.cloned.1.call-done = f32[96,896]{1,0:T(8,128)} async-done(((f32[768,896]{1,0:T(8,128)}), f32[96,896]{1,0:T(8,128)}) %reduce-scatter.5.cloned.1.call-update) | async-done | bytes 344080 | tf_op jit(solution)/shard_map/reduce_scatter | solution.py:83
  185.4 1.3 fusion.21
  186.7 35.2 %all-reduce.6 = (f32[768]{0:T(1024)S(1)}, f32[768]{0:T(1024)S(1)}, f32[896]{0:T(1024)S(1)}) all-reduce(f32[768]{0:T(1024)S(1)} %get-tuple-element.32, f32[768]{0:T(1024)S(1)} %get-tuple-element.6, f32[896]{0:T(1024)S(1)} %broadcast_reduce_fusion), channel_id=3, replica_groups=mesh['dp'=8,'seq'=4] {'dp'}, use_global_device_ids=true, to_apply=%region_7.0.clone | all-reduce | flops 2432 | bytes 19456
  222.2 27.0 %reduce-scatter.7.cloned.1.call-done = f32[96,60]{1,0:T(8,128)} async-done(((f32[768,60]{1,0:T(8,128)}), f32[96,60]{1,0:T(8,128)}) %reduce-scatter.7.cloned.1.call-update) | async-done | bytes 23056
  249.1 1.2 reshape.130
  250.7 10.9 %all-reduce.7 = (f32[15,4,96]{2,1,0:T(4,128)}, f32[96]{0:T(128)}, f32[96]{0:T(128)}, f32[112]{0:T(128)}) all-reduce(f32[15,4,96]{2,1,0:T(4,128)S(1)} %copy.19, f32[96]{0:T(128)S(1)} %dynamic-slice.4, f32[96]{0:T(128)S(1)} %dynamic-slice.6, f32[112]{0:T(128)S(1)} %dynamic-slice.8), channel_id=1, replica_groups=mesh['dp'=8,'seq'=4] {'seq'}, use_global_device_ids=true, to_apply=%region_3.0 | all-reduce | flops 6064 | bytes 48512 | tf_op jit(solution)/shard_map/psum | solution.py:75
  261.6 21.0 %all-reduce.11.cloned.1.call-done = f32[96,896]{1,0:T(8,128)} async-done(((f32[96,896]{1,0:T(8,128)}), f32[96,896]{1,0:T(8,128)}) %all-reduce.11.cloned.1.call-update) | async-done | bytes 344080 | tf_op jit(solution)/shard_map/psum | solution.py:75
  282.6 1.7 copy.41
  (51 shorter events, 7.6 us)
Async XLA Ops:
  7.2 12.4 %copy-start.6 = (bf16[96]{0:T(256)(128)(2,1)S(1)}, bf16[96]{0:T(256)(128)(2,1)}, u32[]{:S(2)}) copy-start(bf16[96]{0:T(256)(128)(2,1)} %param.9) | copy-start | bytes 580
  7.2 12.6 %copy-start.7 = (bf16[96]{0:T(256)(128)(2,1)S(1)}, bf16[96]{0:T(256)(128)(2,1)}, u32[]{:S(2)}) copy-start(bf16[96]{0:T(256)(128)(2,1)} %param.10) | copy-start | bytes 580
  7.2 12.8 %copy-start.8 = (bf16[112]{0:T(256)(128)(2,1)S(1)}, bf16[112]{0:T(256)(128)(2,1)}, u32[]{:S(2)}) copy-start(bf16[112]{0:T(256)(128)(2,1)} %param.12) | copy-start | bytes 676
  7.2 38.4 %copy-start.4 = (bf16[15,4,96]{2,1,0:T(4,128)(2,1)S(1)}, bf16[15,4,96]{2,1,0:T(4,128)(2,1)}, u32[]{:S(2)}) copy-start(bf16[15,4,96]{2,1,0:T(4,128)(2,1)} %param.8) | copy-start | bytes 34564
  7.2 111.4 %all-gather.2.cloned.1.call-start = ((), (), s32[]{:S(2)}) async-start(), calls=%async_computation.2 | async-start | bytes 1548288 | tf_op jit(solution)/shard_map/all_gather | solution.py:29
  7.9 177.5 %reduce-scatter.5.cloned.1.call-start = ((), (), s32[]{:S(2)}) async-start(), calls=%async_computation.3 | async-start | bytes 3096576 | tf_op jit(solution)/shard_map/reduce_scatter | solution.py:83
  9.3 83.3 %collective-permute-start.1 = (s32[1,7]{1,0:T(1,128)}, s32[1,7]{1,0:T(1,128)}, u32[]{:S(2)}, u32[]{:S(2)}) collective-permute-start(s32[1,7]{1,0:T(1,128)} %get-tuple-element.39), channel_id=1, source_target_pairs={{1,0},{2,1},{3,2},{5,4},{6,5},{7,6},{9,8},{10,9},{11,10},{13,12},{... | collective-permute-start | bytes 92 | tf_op jit(solution)/shard_map/ppermute | solution.py:15
  10.6 82.0 %collective-permute-start = (s32[1,7]{1,0:T(1,128)}, s32[1,7]{1,0:T(1,128)}, u32[]{:S(2)}, u32[]{:S(2)}) collective-permute-start(s32[1,7]{1,0:T(1,128)} %get-tuple-element.40), channel_id=1, source_target_pairs={{0,1},{1,2},{2,3},{4,5},{5,6},{6,7},{8,9},{9,10},{10,11},{12,13},{... | collective-permute-start | bytes 92 | tf_op jit(solution)/shard_map/ppermute | solution.py:14
  95.4 14.6 %copy-start.3 = (f32[768]{0:T(1024)S(1)}, f32[768]{0:T(1024)}, u32[]{:S(2)}) copy-start(f32[768]{0:T(1024)} %convert_element_type.79) | copy-start | bytes 9220
  108.6 1.4 copy-start
  110.0 8.3 %copy-start.5 = (bf16[896]{0:T(1024)(128)(2,1)S(1)}, bf16[896]{0:T(1024)(128)(2,1)}, u32[]{:S(2)}) copy-start(bf16[896]{0:T(1024)(128)(2,1)} %get-tuple-element.29) | copy-start | bytes 5380
  116.8 132.4 %reduce-scatter.7.cloned.1.call-start = ((), (), s32[]{:S(2)}) async-start(), calls=%async_computation.5 | async-start | bytes 442368
  118.6 8.5 %copy-start.1 = (bf16[1536,768]{1,0:T(8,128)(2,1)S(1)}, bf16[1536,768]{1,0:T(8,128)(2,1)}, u32[]{:S(2)}) copy-start(bf16[1536,768]{1,0:T(8,128)(2,1)} %copy-done) | copy-start | bytes 7077892
  127.1 1.5 copy-start.2
  139.9 142.7 %all-reduce.11.cloned.1.call-start = ((), (), s32[]{:S(2)}) async-start(), calls=%async_computation.4 | async-start | bytes 688128 | tf_op jit(solution)/shard_map/psum | solution.py:75
Sparse Core Ops, SparseCore 0:
  10.2 50.7 all-gather.1
  116.9 68.4 reduce-scatter.4
  188.7 60.4 reduce-scatter.6
  251.3 31.1 all-reduce.10
where the time goes:
time: 292 us; the launch traced here: 291 us
  blocking collectives  103 us (35%)
  waiting for transfers between devices  70.4 us (24%)
  local copies, waits for them, and re-layouts  46.7 us (16%)
  other arithmetic  24.7 us (8%)
  matrix products  24.3 us (8%)
  between operations  16.6 us (6%)
  starting transfers between devices  5.46 us (2%)
    unnamed x2, blocking collectives  59.4 us
    all_gather x1, blocking collectives, local(): lax.all_gather(embed_weight, 'dp', axis=2, tiled=True)  32.4 us
    unnamed x5, waiting for transfers between devices  27.7 us
    reduce_scatter x1, waiting for transfers between devices, local(): lax.psum_scatter(whole[3], 'dp', scatter_dimension=0, tiled=True)  21.7 us
    psum x1, waiting for transfers between devices, local(): lax.psum((grad_embed_weight, grad_embed_bias, grad_norm_gain, grad_proj_w...  21 us
    unnamed x34, local copies, waits for them, and re-layouts  18.4 us
    psum x1, blocking collectives, local(): lax.psum((grad_embed_weight, grad_embed_bias, grad_norm_gain, grad_proj_w...  10.9 us
    reduce_sum x1, other arithmetic, local(): jnp.mean(mixed.reshape(row_count // 2, 2, -1), axis=1).astype(jnp.bfloat16)  9.17 us
  transfers between devices with their start and end apart: 6, of which 3 were waited for; matrix products, arithmetic and copies ran while one was open for 32% of the time, Pallas kernels for 0%

commit v1 on v0

v1 whole, which is shorter than its diff:
```python
import functools

import jax
import jax.numpy as jnp
from jax import lax
from jax.experimental import pallas as pl
from jax.experimental.pallas import tpu as pltpu
from jax.sharding import PartitionSpec as P

F32, BF16 = jnp.float32, jnp.bfloat16
CUBIC = 0.044715
ROOT = 0.7978845608028654
NT = (((1,), (1,)), ((), ()))
TN = (((0,), (0,)), ((), ()))


def dot(a, b, dims):
    return lax.dot_general(a, b, dims, preferred_element_type=F32)


def build_features(codes_ref, halo_ref, stack_ref, feat_ref, kernel_width):
    half = codes_ref.shape[1]
    ext = jnp.concatenate([halo_ref[0], codes_ref[...], halo_ref[1]], axis=1)
    total = half + 256
    for parity in range(2):
        for k in range(kernel_width):
            source = parity + k - kernel_width // 2
            row, shift = source % 2, (source - source % 2) // 2
            moved = ext if shift == 0 else pltpu.roll(ext, (-shift) % total, 1)
            stack_ref[parity, k : k + 1, :] = moved[row : row + 1, 128 : 128 + half]
        stack_ref[parity, kernel_width : kernel_width + 1, :] = jnp.ones((1, half), jnp.int32)
        stack = stack_ref[parity]
        for c in range(4):
            feat_ref[parity, 16 * c : 16 * c + 16, :] = (
                jnp.where(stack == c + 1, 1.0, 0.0).astype(BF16)
            )


def pick_row(lane, packed):
    lanes = lax.broadcasted_iota(jnp.int32, (16, 128), 1)
    onehot = jnp.where(lanes == lane, 1.0, 0.0).astype(BF16)
    return dot(onehot, packed, NT)[0:1]


def forward_chunk(start, size, feat_ref, weight, gain, scaled_ref, slope_ref, inv_ref, pact_ref):
    total = None
    for parity in range(2):
        features = feat_ref[parity, :, pl.ds(start, size)]
        emb = dot(features, weight, (((0,), (1,)), ((), ())))
        emb = emb.astype(BF16).astype(F32)
        inverse = lax.rsqrt(jnp.mean(emb * emb, axis=1, keepdims=True) + 1e-6)
        scaled = emb * inverse
        x = scaled * gain
        sq = x * x
        t = jnp.tanh(x * (ROOT + (ROOT * CUBIC) * sq))
        half_x = 0.5 * x
        act = half_x + half_x * t
        half_t = 0.5 + 0.5 * t
        slope = half_t + half_x * (1.0 - t * t) * (ROOT + (3.0 * ROOT * CUBIC) * sq)
        scaled_ref[parity, pl.ds(start, size), :] = scaled
        slope_ref[parity, pl.ds(start, size), :] = slope
        inv_ref[parity, pl.ds(start, size), :] = jnp.broadcast_to(inverse, (size, 128))
        total = act if total is None else total + act
    pact_ref[pl.ds(start, size), :] = total.astype(BF16)


def backward_chunk(start, size, cot_ref, w, gain, scaled_ref, slope_ref, inv_ref, ge_ref, gain_acc):
    ga = dot(cot_ref[pl.ds(start, size), :], w, NT)
    width = ga.shape[1]
    for parity in range(2):
        scaled = scaled_ref[parity, pl.ds(start, size), :]
        inverse = inv_ref[parity, pl.ds(start, size), 0:1]
        u = ga * slope_ref[parity, pl.ds(start, size), :]
        q = u * scaled
        gain_acc[...] += jnp.sum(q.reshape(size // 8, 8, width), axis=0)
        mean = jnp.sum(q * gain, axis=1, keepdims=True) * (1.0 / width)
        ge = inverse * (u * gain - scaled * mean)
        ge_ref[parity, pl.ds(start, size), :] = ge.astype(BF16)


def small_grads(feat_ref, ge_ref, cot_ref, gain_acc, put):
    g = dot(feat_ref[0], ge_ref[0], (((1,), (0,)), ((), ())))
    g = g + dot(feat_ref[1], ge_ref[1], (((1,), (0,)), ((), ())))
    width = g.shape[1]
    gain_row = jnp.sum(gain_acc[...], axis=0, keepdims=True)
    rows = lax.broadcasted_iota(jnp.int32, (64, width), 0)
    low = jnp.where(rows == 0, gain_row, 0.0)
    channels = jnp.concatenate([g, low], axis=0).T
    ones = jnp.ones((16, cot_ref.shape[0]), BF16)
    pb = 2.0 * dot(ones, cot_ref[...], (((1,), (0,)), ((), ())))[0:1]
    rows = lax.broadcasted_iota(jnp.int32, (128, pb.shape[1]), 0)
    biases = jnp.where(rows == 65, pb, 0.0).T
    return channels, biases


def local_kernel(dp, kernel_width, codes_ref, halo_ref, packed_ref, w_ref, cot_ref,
                 pooled_ref, gw_ref, small_ref,
                 stack, feat, scaled, slope, inv, pact, ge, gain_acc):
    half = codes_ref.shape[1]
    d0, d1 = w_ref.shape
    part0, part1 = d0 // dp, d1 // dp
    build_features(codes_ref, halo_ref, stack, feat, kernel_width)
    channels = jnp.concatenate([packed_ref[d, :part0, :] for d in range(dp)], axis=0)
    weight = channels[:, :64]
    gain = pick_row(64, channels)
    bias = pick_row(65, jnp.concatenate([packed_ref[d] for d in range(dp)], axis=0))
    gain_acc[...] = jnp.zeros_like(gain_acc)
    size = 128

    @pl.loop(0, half // size)
    def _(i):
        start = pl.multiple_of(i * size, size)
        forward_chunk(start, size, feat, weight, gain, scaled, slope, inv, pact)

    @pl.loop(0, d0 // 128)
    def _(i):
        start = pl.multiple_of(i * 128, 128)
        gw_ref[pl.ds(start, 128), :] = dot(pact[:, pl.ds(start, 128)], cot_ref[...], TN).astype(BF16)

    w = w_ref[...]

    @pl.loop(0, half // size)
    def _(i):
        start = pl.multiple_of(i * size, size)
        pooled = 0.5 * dot(pact[pl.ds(start, size), :], w, (((1,), (0,)), ((), ()))) + bias
        pooled_ref[pl.ds(start, size), :] = pooled.astype(BF16)

    @pl.loop(0, half // size)
    def _(i):
        start = pl.multiple_of(i * size, size)
        backward_chunk(start, size, cot_ref, w, gain, scaled, slope, inv, ge, gain_acc)

    chan, biases = small_grads(feat, ge, cot_ref, gain_acc, None)
    for d in range(dp):
        own = biases[d * part1 : (d + 1) * part1]
        small_ref[d, :part0, :] = own[:part0] + chan[d * part0 : (d + 1) * part0]
        small_ref[d, part0:, :] = own[part0:]


def shape(dims, kind):
    return jax.ShapeDtypeStruct(dims, kind)


def local(dp, seq, bases, embed_weight, embed_bias, norm_gain, proj_weight, proj_bias, cotangent):
    kernel_width, letters, part0 = embed_weight.shape
    part1 = proj_bias.shape[0]
    d0, d1 = part0 * dp, part1 * dp
    half = bases.shape[1] // 2
    codes = jnp.pad((bases[0] + 1).reshape(half, 2).T, ((0, 6), (0, 0)))
    lanes = jnp.pad(
        embed_weight.transpose(2, 1, 0), ((0, 0), (0, 0), (0, 16 - kernel_width))
    )
    lanes = lanes.at[:, 0, 15].set(embed_bias).reshape(part0, 64)
    packed = jnp.concatenate([lanes, norm_gain[:, None]], axis=1)
    packed = jnp.pad(packed, ((0, part1 - part0), (0, 63)))
    packed = packed.at[:, 65].set(proj_bias)
    up = [(i, i + 1) for i in range(seq - 1)]
    before = lax.ppermute(codes[:, half - 128 :], "seq", up)
    after = lax.ppermute(codes[:, :128], "seq", [(j, i) for i, j in up])
    halo = jnp.stack([before, after])
    packs = lax.all_gather(packed, "dp", axis=0)
    w = lax.all_gather(proj_weight, "dp", axis=0, tiled=True)
    vmem = pl.BlockSpec(memory_space=pltpu.VMEM)
    pooled, gw, small = pl.pallas_call(
        functools.partial(local_kernel, dp, kernel_width),
        out_shape=(shape((half, d1), BF16), shape((d0, d1), BF16), shape((dp, part1, 128), F32)),
        in_specs=[vmem] * 5,
        out_specs=(vmem,) * 3,
        scratch_shapes=[
            pltpu.VMEM((2, 16, half), jnp.int32),
            pltpu.VMEM((2, 64, half), BF16),
            pltpu.VMEM((2, half, d0), F32),
            pltpu.VMEM((2, half, d0), F32),
            pltpu.VMEM((2, half, 128), F32),
            pltpu.VMEM((half, d0), BF16),
            pltpu.VMEM((2, half, d0), BF16),
            pltpu.VMEM((8, d0), F32),
        ],
        compiler_params=pltpu.CompilerParams(vmem_limit_bytes=50 * 2**20),
        name="fused_step",
    )(codes, halo, packs, w, cotangent[0])
    gw = lax.psum(lax.psum_scatter(gw, "dp", scatter_dimension=0, tiled=True), "seq")
    small = lax.psum(lax.psum_scatter(small, "dp", scatter_dimension=0), "seq")
    return finish(pooled, gw, small, kernel_width, part0, half * seq * dp)


def finish(pooled, gw, small, kernel_width, part0, pairs):
    factor = 0.25 / pairs
    small = small * factor
    embed = small[:part0, :64].reshape(part0, 4, 16)
    return (
        pooled[None],
        embed[:, :, :kernel_width].transpose(2, 1, 0),
        embed[:, 0, 15],
        small[:part0, 64],
        gw.astype(F32) * factor,
        small[:, 65],
    )


def solution(mesh):
    placed = (
        P("dp", "seq"),
        P(None, None, "dp"),
        P("dp"),
        P("dp"),
        P("dp", None),
        P("dp"),
        P("dp", "seq", None),
    )
    return jax.shard_map(
        functools.partial(local, mesh.shape["dp"], mesh.shape["seq"]),
        mesh=mesh,
        in_specs=placed,
        out_specs=(
            P("dp", "seq", None),
            P(None, None, "dp"),
            P("dp"),
            P("dp"),
            P("dp", None),
            P("dp"),
        ),
        check_vma=False,
    )
```

time: 292 us -> 248 us (0.85)
  waiting for transfers between devices: 70.4 us -> 152 us
  blocking collectives: 103 us -> 43.6 us
  local copies, waits for them, and re-layouts: 46.7 us -> 7.21 us
  matrix products: 24.3 us -> 0 us
  Pallas kernels: 0 us -> 17.9 us
  other arithmetic: 24.7 us -> 9 us
    reduce_scatter x1 -> x2, waiting for transfers between devices: 21.7 us -> 117 us  [the longest x1 62.5 us: local(): small = lax.psum(lax.psum_scatter(small, 'dp', scatter_dimension=0), 'seq')]
    unnamed x2 -> x0, blocking collectives: 59.4 us -> none
    unnamed x5 -> x4, waiting for transfers between devices: 27.7 us -> 1.39 us
    dot_general x5 -> x0, matrix products: 24.3 us -> none  [the longest x1 8.43 us: local(): lax.dot_general(grad_mixed, full_proj, (((1,), (1,)), ((), ())), preferre...]
    pallas_call x0 -> x1, Pallas kernels: none -> 17.9 us  [local(): pl.pallas_call(functools.partial(local_kernel, dp, kernel_width), out_sha...]
    unnamed x34 -> x4, local copies, waits for them, and re-layouts: 18.4 us -> 2.69 us
    reduce_sum x3 -> x0, other arithmetic: 10.9 us -> none  [the longest x1 9.17 us: local(): jnp.mean(mixed.reshape(row_count // 2, 2, -1), axis=1).astype(jnp.bfloat16)]
    psum x1, waiting for transfers between devices: 21 us -> 30.9 us  [local(): lax.psum(lax.psum_scatter(gw, 'dp', scatter_dimension=0, tiled=True), 'seq')]
  transfers between devices with their start and end apart: 6 -> 6, of which waited for: 3 -> 4; matrix products, arithmetic and copies ran while one was open for 32% -> 5% of each run, Pallas kernels for 0% -> 0%
where the time goes in v1:
time: 248 us; the launch traced here: 247 us
  waiting for transfers between devices  152 us (61%)
  blocking collectives  43.6 us (18%)
  Pallas kernels  17.9 us (7%)
  between operations  13.9 us (6%)
  other arithmetic  9 us (4%)
  local copies, waits for them, and re-layouts  7.21 us (3%)
  starting transfers between devices  3.81 us (2%)
    reduce_scatter x1, waiting for transfers between devices, local(): small = lax.psum(lax.psum_scatter(small, 'dp', scatter_dimension=0), 'seq')  62.5 us
    reduce_scatter x1, waiting for transfers between devices, local(): lax.psum_scatter(gw, 'dp', scatter_dimension=0, tiled=True)  54.9 us
    all_gather x1, blocking collectives, local(): packs = lax.all_gather(packed, 'dp', axis=0)  32.4 us
    psum x1, waiting for transfers between devices, local(): lax.psum(lax.psum_scatter(gw, 'dp', scatter_dimension=0, tiled=True), 'seq')  30.9 us
    pallas_call x1, Pallas kernels, local(): pl.pallas_call(functools.partial(local_kernel, dp, kernel_width), out_sha...  17.9 us
    psum x1, blocking collectives, local(): small = lax.psum(lax.psum_scatter(small, 'dp', scatter_dimension=0), 'seq')  11.2 us
  transfers between devices with their start and end apart: 6, of which 4 were waited for; matrix products, arithmetic and copies ran while one was open for 5% of the time, Pallas kernels for 0%

profile of v1, /device:TPU:0, one launch (start us, length us, event | category | flops | bytes accessed | tf_op | source)
XLA Modules:
  0.0 247.2 jit_solution(1713761678946185081)
XLA Ops:
  7.2 0.7 all-gather.2.cloned.1.call-update
  7.9 0.7 add_reduce_fusion
  8.7 0.3 add.30
  9.0 0.1 copy.26
  9.2 2.4 collective-permute-start
  11.5 1.3 collective-permute-start.1
  12.8 0.7 copy.32
  13.6 0.6 fusion.8
  14.1 1.4 and_reduce_fusion
  15.5 2.6 %broadcast_select_fusion.1 = bf16[96,1,1]{0,2,1:T(2,128)(2,1)S(1)} fusion(pred[]{:T(512)} %and_reduce_fusion, bf16[96]{0:T(256)(128)(2,1)} %param.13, s32[]{:T(128)} %bitcast.5, s32[]{:T(128)} %bitcast.6, bf16[96,4,15]{0,2,1:T(8,128)(2,1)S(1)} %bitcast.26), kind=kLoop, calls=%fused_computation.22 | loop fusion | flops 96 | bytes 11913 | tf_op jit(solution)/shard_map/select.2
  18.1 1.3 scatter.6
  19.4 0.6 compare_reduce_fusion
  20.1 0.7 fusion.6
  20.8 1.3 fusion.7
  22.1 0.1 copy.28
  22.2 32.4 %all_gather.13.packed_ref = bf16[8,112,128]{2,1,0:T(8,128)(2,1)S(1)} all-gather(bf16[1,112,128]{2,1,0:T(8,128)(2,1)S(1)} %copy.28), channel_id=1, replica_groups=mesh['dp'=8,'seq'=4] {'dp'}, dimensions={0}, use_global_device_ids=true | all-gather | bytes 258048 | tf_op jit(solution)/shard_map/all_gather | solution.py:161
  54.7 2.1 all-gather.2.cloned.1.call-done.w_ref
  56.8 1.3 copy-done
  58.1 17.9 %fused_step.1 = (bf16[768,896]{1,0:T(8,128)(2,1)}, bf16[768,896]{1,0:T(8,128)(2,1)}, f32[8,112,128]{2,1,0:T(8,128)}) custom-call(s32[8,768]{1,0:T(8,128)S(1)} %pad.17.codes_ref, s32[2,8,128]{2,1,0:T(8,128)S(1)} %pad_add_fusion.halo_ref, bf16[8,112,128]{2,1,0:T(8,128)(2,1)S(1)} %all_gather.13.packed_ref, bf16[768,896]{1,0:T(8,128)(2,1)S(1)} %copy-done, ...), custom_call_target="tpu_custom_call" | custom-call | tf_op jit(solution)/shard_map/fused_step/pallas_call | solution.py:164
  76.1 0.0 reduce-scatter.5.cloned.1.call-start
  76.1 0.7 reduce-scatter.5.cloned.1.call-update
  76.8 0.0 all-reduce.5.cloned.1.call-start
  76.9 62.5 %reduce-scatter.3.cloned.1.call-done = f32[1,112,128]{2,1,0:T(8,128)} async-done(((f32[8,112,128]{2,1,0:T(8,128)}), f32[1,112,128]{2,1,0:T(8,128)}) %reduce-scatter.3.cloned.1.call-update) | async-done | bytes 57360 | tf_op jit(solution)/shard_map/reduce_scatter | solution.py:183
  139.3 11.2 %psum.14 = f32[112,128]{1,0:T(8,128)S(1)} all-reduce(f32[112,128]{1,0:T(8,128)} %bitcast.30), channel_id=1, replica_groups=mesh['dp'=8,'seq'=4] {'seq'}, use_global_device_ids=true, to_apply=%region_3.4 | all-reduce | flops 14336 | bytes 114688 | tf_op jit(solution)/shard_map/psum | solution.py:183
  150.5 0.1 copy.29
  150.6 0.6 copy.30
  151.3 0.7 slice_reduce_fusion
  152.0 0.5 slice_bitcast_fusion.1
  152.5 54.9 %reduce-scatter.5.cloned.1.call-done = bf16[96,896]{1,0:T(8,128)(2,1)} async-done(((bf16[768,896]{1,0:T(8,128)(2,1)}), bf16[96,896]{1,0:T(8,128)(2,1)}) %reduce-scatter.5.cloned.1.call-update) | async-done | bytes 172048 | tf_op jit(solution)/shard_map/reduce_scatter | solution.py:182
  207.4 0.7 slice_reduce_fusion.1
  208.1 30.9 %all-reduce.5.cloned.1.call-done = bf16[96,896]{1,0:T(8,128)(2,1)} async-done(((bf16[96,896]{1,0:T(8,128)(2,1)}), bf16[96,896]{1,0:T(8,128)(2,1)}) %all-reduce.5.cloned.1.call-update) | async-done | bytes 172048 | tf_op jit(solution)/shard_map/psum | solution.py:182
  238.9 1.7 convert_multiply_fusion
  (16 shorter events, 0.2 us)
Async XLA Ops:
  7.2 49.6 %all-gather.2.cloned.1.call-start = ((), (), s32[]{:S(2)}) async-start(), calls=%async_computation.2 | async-start | bytes 1548288 | tf_op jit(solution)/shard_map/all_gather | solution.py:162
  7.9 131.4 %reduce-scatter.3.cloned.1.call-start = ((), (), s32[]{:S(2)}) async-start(), calls=%async_computation.3 | async-start | bytes 516096 | tf_op jit(solution)/shard_map/reduce_scatter | solution.py:183
  9.2 45.5 %collective-permute-start = (s32[8,128]{1,0:T(8,128)S(1)}, s32[8,128]{1,0:T(8,128)S(1)}, u32[]{:S(2)}, u32[]{:S(2)}) collective-permute-start(s32[8,128]{1,0:T(8,128)S(1)} %get-tuple-element.48), channel_id=1, source_target_pairs={{0,1},{1,2},{2,3},{4,5},{5,6},{6,7},{8,9},{9,10},{10,11},{12,13},{... | collective-permute-start | bytes 12296 | tf_op jit(solution)/shard_map/ppermute | solution.py:158
  11.5 43.1 %collective-permute-start.1 = (s32[8,128]{1,0:T(8,128)S(1)}, s32[8,128]{1,0:T(8,128)S(1)}, u32[]{:S(2)}, u32[]{:S(2)}) collective-permute-start(s32[8,128]{1,0:T(8,128)S(1)} %get-tuple-element.49), channel_id=1, source_target_pairs={{1,0},{2,1},{3,2},{5,4},{6,5},{7,6},{9,8},{10,9},{11,10},{13,12},{... | collective-permute-start | bytes 12296 | tf_op jit(solution)/shard_map/ppermute | solution.py:159
  56.8 1.3 copy-start
  76.1 131.3 %reduce-scatter.5.cloned.1.call-start = ((), (), s32[]{:S(2)}) async-start(), calls=%async_computation.4 | async-start | bytes 1548288 | tf_op jit(solution)/shard_map/reduce_scatter | solution.py:182
  76.8 162.1 %all-reduce.5.cloned.1.call-start = ((), (), s32[]{:S(2)}) async-start(), calls=%async_computation.5 | async-start | bytes 344064 | tf_op jit(solution)/shard_map/psum | solution.py:182
Sparse Core Ops, SparseCore 0:
  10.2 46.5 all-gather.1
  76.2 63.0 reduce-scatter.2
  143.1 64.1 reduce-scatter.4
  209.7 29.2 all-reduce.4

commit v2 on v1

--- a/solution.py
+++ b/solution.py
@@ -78,18 +78,18 @@
         ge_ref[parity, pl.ds(start, size), :] = ge.astype(BF16)
 
 
-def small_grads(feat_ref, ge_ref, cot_ref, gain_acc, put):
+def small_grads(feat_ref, ge_ref, cot_ref, gain_acc):
     g = dot(feat_ref[0], ge_ref[0], (((1,), (0,)), ((), ())))
     g = g + dot(feat_ref[1], ge_ref[1], (((1,), (0,)), ((), ())))
     width = g.shape[1]
     gain_row = jnp.sum(gain_acc[...], axis=0, keepdims=True)
     rows = lax.broadcasted_iota(jnp.int32, (64, width), 0)
-    low = jnp.where(rows == 0, gain_row, 0.0)
-    channels = jnp.concatenate([g, low], axis=0).T
+    g = jnp.where(rows == 31, gain_row, g)
+    channels = jnp.concatenate([g, jnp.zeros_like(g)], axis=0).T
     ones = jnp.ones((16, cot_ref.shape[0]), BF16)
     pb = 2.0 * dot(ones, cot_ref[...], (((1,), (0,)), ((), ())))[0:1]
     rows = lax.broadcasted_iota(jnp.int32, (128, pb.shape[1]), 0)
-    biases = jnp.where(rows == 65, pb, 0.0).T
+    biases = jnp.where(rows == 64, pb, 0.0).T
     return channels, biases
 
 
@@ -102,8 +102,8 @@
     build_features(codes_ref, halo_ref, stack, feat, kernel_width)
     channels = jnp.concatenate([packed_ref[d, :part0, :] for d in range(dp)], axis=0)
     weight = channels[:, :64]
-    gain = pick_row(64, channels)
-    bias = pick_row(65, jnp.concatenate([packed_ref[d] for d in range(dp)], axis=0))
+    gain = pick_row(31, channels)
+    bias = pick_row(64, jnp.concatenate([packed_ref[d] for d in range(dp)], axis=0))
     gain_acc[...] = jnp.zeros_like(gain_acc)
     size = 128
 
@@ -130,15 +130,295 @@
         start = pl.multiple_of(i * size, size)
         backward_chunk(start, size, cot_ref, w, gain, scaled, slope, inv, ge, gain_acc)
 
-    chan, biases = small_grads(feat, ge, cot_ref, gain_acc, None)
+    chan, biases = small_grads(feat, ge, cot_ref, gain_acc)
     for d in range(dp):
         own = biases[d * part1 : (d + 1) * part1]
         small_ref[d, :part0, :] = own[:part0] + chan[d * part0 : (d + 1) * part0]
         small_ref[d, part0:, :] = own[part0:]
 
 
+MESH = pl.DeviceIdType.MESH
+
+
+def fused_kernel(kernel_width, codes_ref, rows_ref, w_ref, cot_hbm,
+                 pooled_hbm, gw_ref, small_out,
+                 halo, stack, feat, scaled, slope, inv, pact, ge, gain_acc,
+                 pack, packs, wbuf, cot, pooled, gwb, s1buf, p1, s2buf, sum2, s3buf, fin,
+                 small, sbuf, tbuf,
+                 send_sem, halo_recv, pack_recv, w_recv, s1_recv, s2_recv, s3_recv, fin_recv,
+                 small_recv, t_recv, local_sem):
+    dp, seq = 8, 4
+    half = codes_ref.shape[1]
+    part0, d1 = w_ref.shape
+    d0, part1, part_h = part0 * dp, d1 // dp, part0 // 2
+    me, pos = lax.axis_index("dp"), lax.axis_index("seq")
+    z, y, x, c = me // 2, me % 2, pos // 2, pos % 2
+    y2, x2, c2 = 1 - y, 1 - x, 1 - c
+    own_rank = z % 2 == x
+    factor = 0.25 / (half * seq * dp)
+
+    cot_in = pltpu.make_async_copy(cot_hbm, cot, local_sem.at[0])
+    cot_in.start()
+
+    pack[...] = rows_ref[...].T[:part1].astype(BF16)
+    packs[me] = pack[...]
+    wbuf[me] = w_ref[...].reshape(2, part_h, d1)
+
+    barrier = pltpu.get_barrier_semaphore()
+    for j in range(1, dp):
+        pl.semaphore_signal(
+            barrier, inc=1, device_id={"dp": (me + j) % dp, "seq": pos}, device_id_type=MESH
+        )
+    for j in range(1, seq):
+        pl.semaphore_signal(
+            barrier, inc=1, device_id={"dp": me, "seq": (pos + j) % seq}, device_id_type=MESH
+        )
+        pl.semaphore_signal(
+            barrier,
+            inc=1,
+            device_id={"dp": 2 * z + y2, "seq": (pos + j) % seq},
+            device_id_type=MESH,
+        )
+    pl.semaphore_wait(barrier, dp - 1 + 2 * (seq - 1))
+
+    started = []
+
+    def send(src, dst, recv, to_dp, to_seq, pred=None):
+        copy = pltpu.make_async_remote_copy(
+            src_ref=src, dst_ref=dst, send_sem=send_sem.at[len(started)], recv_sem=recv,
+            device_id={"dp": to_dp, "seq": to_seq}, device_id_type=MESH,
+        )
+        started.append((copy, pred))
+        if pred is None:
+            copy.start()
+        else:
+            pl.when(pred)(lambda: copy.start())
+
+    def arrive(dst, recv, pred=None):
+        copy = pltpu.make_async_remote_copy(
+            src_ref=dst, dst_ref=dst, send_sem=send_sem.at[0], recv_sem=recv,
+            device_id={"dp": me, "seq": (pos + 1) % seq}, device_id_type=MESH,
+        )
+        if pred is None:
+            copy.wait_recv()
+        else:
+            pl.when(pred)(lambda: copy.wait_recv())
+
+    for j in range(1, dp):
+        send(pack, packs.at[me], pack_recv.at[me], (me + j) % dp, pos)
+    send(codes_ref.at[:, half - 128 :], halo.at[0], halo_recv.at[0], me, pos + 1, pos < seq - 1)
+    send(codes_ref.at[:, :128], halo.at[1], halo_recv.at[1], me, pos - 1, pos > 0)
+    for zz in range(4):
+        send(wbuf.at[me, c], wbuf.at[me, c], w_recv.at[me, c], 2 * zz + y, pos,
+             own_rank & (z != zz))
+    send(wbuf.at[me, c], wbuf.at[me, c], w_recv.at[me, c], 2 * z + y2, pos)
+
+    gain_acc[...] = jnp.zeros_like(gain_acc)
+    arrive(halo.at[0], halo_recv.at[0], pos > 0)
+    arrive(halo.at[1], halo_recv.at[1], pos < seq - 1)
+
+    @pl.when(pos == 0)
+    def _():
+        halo[0] = jnp.zeros(halo.shape[1:], jnp.int32)
+
+    @pl.when(pos == seq - 1)
+    def _():
+        halo[1] = jnp.zeros(halo.shape[1:], jnp.int32)
+
+    build_features(codes_ref, halo, stack, feat, kernel_width)
+    for j in range(1, dp):
+        arrive(packs.at[(me + j) % dp], pack_recv.at[(me + j) % dp])
+    channels = jnp.concatenate([packs[d, :part0, :] for d in range(dp)], axis=0)
+    weight = channels[:, :64]
+    gain = pick_row(31, channels)
+    bias = pick_row(64, packs[...].reshape(dp * part1, 128))
+    size = 128
+    chunks = half // size
+
+    def forward(first, last):
+        @pl.loop(first, last)
+        def _(i):
+            start = pl.multiple_of(i * size, size)
+            forward_chunk(start, size, feat, weight, gain, scaled, slope, inv, pact)
+
+    forward(0, chunks // 3)
+    for zz in range(4):
+        d = 2 * zz + y
+        slot, sem = wbuf.at[d, c], w_recv.at[d, c]
+        other = z != zz
+        direct = other & (x == zz % 2)
+        arrive(slot, sem, direct)
+        send(slot, slot, sem, 2 * z + y2, pos, direct)
+        send(slot, slot, sem, me, 2 * x2 + c, direct)
+        send(slot, slot, sem, 2 * z + y2, 2 * x2 + c, direct)
+        send(slot, slot, sem, me, 2 * x + c2, direct)
+    d = 2 * z + y2
+    arrive(wbuf.at[d, c], w_recv.at[d, c])
+    send(wbuf.at[d, c], wbuf.at[d, c], w_recv.at[d, c], me, 2 * x + c2)
+    forward(chunks // 3, chunks)
+    for zz in range(4):
+        d = 2 * zz + y
+        slot, sem = wbuf.at[d, c], w_recv.at[d, c]
+        relayed = (z != zz) & (x != zz % 2)
+        arrive(slot, sem, relayed)
+        send(slot, slot, sem, me, 2 * x + c2, relayed)
+        d = 2 * zz + y2
+        slot, sem = wbuf.at[d, c], w_recv.at[d, c]
+        arrive(slot, sem, z != zz)
+        send(slot, slot, sem, me, 2 * x + c2, z != zz)
+
+    cot_in.wait()
+    block = d0 // 2
+    for b in range(2):
+        value = dot(pact[:, b * block : (b + 1) * block], cot[...], TN)
+        gwb[4 * b : 4 * b + 4] = value.astype(BF16).reshape(4, 2, part_h, d1)
+        send(gwb.at[4 * b : 4 * b + 4, c2], s1buf.at[b], s1_recv.at[b], me, 2 * x + c2)
+
+    for d in range(dp):
+        arrive(wbuf.at[d, c2], w_recv.at[d, c2], me != d)
+
+    @pl.loop(0, chunks)
+    def _(i):
+        start = pl.multiple_of(i * size, size)
+        w = wbuf[...].reshape(d0, d1)
+        value = 0.5 * dot(pact[pl.ds(start, size), :], w, (((1,), (0,)), ((), ()))) + bias
+        pooled[pl.ds(start, size), :] = value.astype(BF16)
+
+    pooled_out = pltpu.make_async_copy(pooled, pooled_hbm, local_sem.at[1])
+    pooled_out.start()
+
+    for b in range(2):
+        arrive(s1buf.at[b], s1_recv.at[b])
+        for k in range(4):
+            p1[b, k] = (gwb[4 * b + k, c].astype(F32) + s1buf[b, k].astype(F32)).astype(BF16)
+    rank = 2 * x + y
+    send(p1.at[:, 2 * x + y2], s2buf.at[rank], s2_recv.at[rank], 2 * z + y2, pos)
+    send(p1.at[:, 2 * x2 + y], s2buf.at[rank], s2_recv.at[rank], me, 2 * x2 + c)
+    send(p1.at[:, 2 * x2 + y2], s2buf.at[rank], s2_recv.at[rank], 2 * z + y2, 2 * x2 + c)
+
+    def backward(first, last):
+        @pl.loop(first, last)
+        def _(i):
+            start = pl.multiple_of(i * size, size)
+            w = wbuf[...].reshape(d0, d1)
+            backward_chunk(start, size, cot, w, gain, scaled, slope, inv, ge, gain_acc)
+
+    backward(0, chunks // 2)
+    total = [p1[k, rank].astype(F32) for k in range(2)]
+    for other in (2 * x + y2, 2 * x2 + y, 2 * x2 + y2):
+        arrive(s2buf.at[other], s2_recv.at[other])
+        total = [total[k] + s2buf[other, k].astype(F32) for k in range(2)]
+    for k in range(2):
+        sum2[k] = total[k].astype(BF16)
+    for k in range(2):
+        zt = x + 2 * k
+        send(sum2.at[k], s3buf.at[z], s3_recv.at[z], 2 * zt + y, pos, zt != z)
+    backward(chunks // 2, chunks)
+
+    chan, biases = small_grads(feat, ge, cot, gain_acc)
+    for d in range(dp):
+        own = biases[d * part1 : (d + 1) * part1]
+        small[d, :part0, :] = (own[:part0] + chan[d * part0 : (d + 1) * part0]).astype(BF16)
+        small[d, part0:, :] = own[part0:].astype(BF16)
+    for j in range(1, dp):
+        to = (me + j) % dp
+        send(small.at[to], sbuf.at[me], small_recv.at[me], to, pos)
+
+    for zz in range(4):
+        arrive(s3buf.at[zz], s3_recv.at[zz], own_rank & (z != zz))
+
+    @pl.when(own_rank)
+    def _():
+        value = sum2[z // 2].astype(F32)
+        for j in range(1, 4):
+            value = value + s3buf[(z + j) % 4].astype(F32)
+        fin[c] = value.astype(BF16)
+
+    for to in (2 * x + c2, 2 * x2 + c, 2 * x2 + c2):
+        send(fin.at[c], fin.at[c], fin_recv.at[c], me, to, own_rank)
+
+    sbuf[me] = small[me]
+    for j in range(1, dp):
+        arrive(sbuf.at[(me + j) % dp], small_recv.at[(me + j) % dp])
+    tbuf[pos] = jnp.sum(sbuf[...].astype(F32), axis=0).astype(BF16)
+    for j in range(1, seq):
+        send(tbuf.at[pos], tbuf.at[pos], t_recv.at[pos], me, (pos + j) % seq)
+
+    arrive(fin.at[c2], fin_recv.at[c2])
+    arrive(fin.at[c], fin_recv.at[c], jnp.logical_not(own_rank))
+    gw_ref[...] = fin[...].astype(F32).reshape(part0, d1) * factor
+    for j in range(1, seq):
+        arrive(tbuf.at[(pos + j) % seq], t_recv.at[(pos + j) % seq])
+    value = jnp.sum(tbuf[...].astype(F32), axis=0) * factor
+    padded = jnp.concatenate([value, jnp.zeros((128 - part1, 128), F32)], axis=0)
+    small_out[...] = padded.T
+
+    for copy, pred in started:
+        if pred is None:
+            copy.wait_send()
+        else:
+            pl.when(pred)(lambda copy=copy: copy.wait_send())
+    pooled_out.wait()
+
+
 def shape(dims, kind):
     return jax.ShapeDtypeStruct(dims, kind)
+
+
+def fused(kernel_width, codes, rows, proj_weight, cot):
+    half = codes.shape[1]
+    part0, d1 = proj_weight.shape
+    dp, seq = 8, 4
+    d0, part1, part_h = part0 * dp, d1 // dp, part0 // 2
+    vmem, hbm = pl.BlockSpec(memory_space=pltpu.VMEM), pl.BlockSpec(memory_space=pl.ANY)
+    dma = pltpu.SemaphoreType.DMA
+    return pl.pallas_call(
+        functools.partial(fused_kernel, kernel_width),
+        out_shape=(shape((half, d1), BF16), shape((part0, d1), F32), shape((128, 128), F32)),
+        in_specs=[vmem, vmem, vmem, hbm],
+        out_specs=(hbm, vmem, vmem),
+        scratch_shapes=[
+            pltpu.VMEM((2, 8, 128), jnp.int32),
+            pltpu.VMEM((2, 16, half), jnp.int32),
+            pltpu.VMEM((2, 64, half), BF16),
+            pltpu.VMEM((2, half, d0), F32),
+            pltpu.VMEM((2, half, d0), F32),
+            pltpu.VMEM((2, half, 128), F32),
+            pltpu.VMEM((half, d0), BF16),
+            pltpu.VMEM((2, half, d0), BF16),
+            pltpu.VMEM((8, d0), F32),
+            pltpu.VMEM((part1, 128), BF16),
+            pltpu.VMEM((dp, part1, 128), BF16),
+            pltpu.VMEM((dp, 2, part_h, d1), BF16),
+            pltpu.VMEM((half, d1), BF16),
+            pltpu.VMEM((half, d1), BF16),
+            pltpu.VMEM((dp, 2, part_h, d1), BF16),
+            pltpu.VMEM((2, 4, part_h, d1), BF16),
+            pltpu.VMEM((2, 4, part_h, d1), BF16),
+            pltpu.VMEM((4, 2, part_h, d1), BF16),
+            pltpu.VMEM((2, part_h, d1), BF16),
+            pltpu.VMEM((4, part_h, d1), BF16),
+            pltpu.VMEM((2, part_h, d1), BF16),
+            pltpu.VMEM((dp, part1, 128), BF16),
+            pltpu.VMEM((dp, part1, 128), BF16),
+            pltpu.VMEM((seq, part1, 128), BF16),
+            dma((72,)),
+            dma((2,)),
+            dma((dp,)),
+            dma((dp, 2)),
+            dma((2,)),
+            dma((4,)),
+            dma((4,)),
+            dma((2,)),
+            dma((dp,)),
+            dma((seq,)),
+            dma((2,)),
+        ],
+        compiler_params=pltpu.CompilerParams(
+            collective_id=0, has_side_effects=True, vmem_limit_bytes=50 * 2**20
+        ),
+        name="fused_step",
+    )(codes, rows, proj_weight, cot)
 
 
 def local(dp, seq, bases, embed_weight, embed_bias, norm_gain, proj_weight, proj_bias, cotangent):
@@ -147,18 +427,36 @@
     d0, d1 = part0 * dp, part1 * dp
     half = bases.shape[1] // 2
     codes = jnp.pad((bases[0] + 1).reshape(half, 2).T, ((0, 6), (0, 0)))
-    lanes = jnp.pad(
-        embed_weight.transpose(2, 1, 0), ((0, 0), (0, 0), (0, 16 - kernel_width))
+    spare = jnp.stack([embed_bias, norm_gain, jnp.zeros_like(norm_gain), jnp.zeros_like(norm_gain)])
+    spare = jnp.pad(spare[:, None], ((0, 0), (0, 16 - kernel_width - 1), (0, 0)))
+    rows = jnp.concatenate([embed_weight.transpose(1, 0, 2), spare], axis=1).reshape(64, part0)
+    rows = jnp.pad(rows, ((0, 0), (0, 128 - part0)))
+    rows = jnp.concatenate([rows, jnp.pad(proj_bias, (0, 128 - part1))[None]], axis=0)
+    rows = jnp.pad(rows.astype(F32), ((0, 63), (0, 0)))
+    if (dp, seq) == (8, 4) and part0 % 32 == 0:
+        pooled, gw, small = fused(kernel_width, codes, rows, proj_weight, cotangent[0])
+    else:
+        pooled, gw, small = separate(dp, seq, kernel_width, codes, rows, proj_weight, cotangent[0])
+    embed = small[:64, :part0].reshape(4, 16, part0)
+    return (
+        pooled[None],
+        embed[:, :kernel_width].transpose(1, 0, 2),
+        small[15, :part0],
+        small[31, :part0],
+        gw,
+        small[64, :part1],
     )
-    lanes = lanes.at[:, 0, 15].set(embed_bias).reshape(part0, 64)
-    packed = jnp.concatenate([lanes, norm_gain[:, None]], axis=1)
-    packed = jnp.pad(packed, ((0, part1 - part0), (0, 63)))
-    packed = packed.at[:, 65].set(proj_bias)
+
+
+def separate(dp, seq, kernel_width, codes, rows, proj_weight, cot):
+    half = codes.shape[1]
+    part0, d1 = proj_weight.shape
+    d0, part1 = part0 * dp, d1 // dp
     up = [(i, i + 1) for i in range(seq - 1)]
     before = lax.ppermute(codes[:, half - 128 :], "seq", up)
     after = lax.ppermute(codes[:, :128], "seq", [(j, i) for i, j in up])
     halo = jnp.stack([before, after])
-    packs = lax.all_gather(packed, "dp", axis=0)
+    packs = lax.all_gather(rows.T[:part1].astype(BF16), "dp", axis=0)
     w = lax.all_gather(proj_weight, "dp", axis=0, tiled=True)
     vmem = pl.BlockSpec(memory_space=pltpu.VMEM)
     pooled, gw, small = pl.pallas_call(
@@ -177,25 +475,13 @@
             pltpu.VMEM((8, d0), F32),
         ],
         compiler_params=pltpu.CompilerParams(vmem_limit_bytes=50 * 2**20),
-        name="fused_step",
-    )(codes, halo, packs, w, cotangent[0])
+        name="local_step",
+    )(codes, halo, packs, w, cot)
     gw = lax.psum(lax.psum_scatter(gw, "dp", scatter_dimension=0, tiled=True), "seq")
     small = lax.psum(lax.psum_scatter(small, "dp", scatter_dimension=0), "seq")
-    return finish(pooled, gw, small, kernel_width, part0, half * seq * dp)
-
-
-def finish(pooled, gw, small, kernel_width, part0, pairs):
-    factor = 0.25 / pairs
-    small = small * factor
-    embed = small[:part0, :64].reshape(part0, 4, 16)
-    return (
-        pooled[None],
-        embed[:, :, :kernel_width].transpose(2, 1, 0),
-        embed[:, 0, 15],
-        small[:part0, 64],
-        gw.astype(F32) * factor,
-        small[:, 65],
-    )
+    factor = 0.25 / (half * seq * dp)
+    small = jnp.pad(small.T * factor, ((0, 0), (0, 128 - part1)))
+    return pooled, gw.astype(F32) * factor, small
 
 
 def solution(mesh):

time: 248 us -> 61.1 us (0.25)
  waiting for transfers between devices: 152 us -> 0 us
  blocking collectives: 43.6 us -> 0 us
  Pallas kernels: 17.9 us -> 50.9 us
  between operations: 13.9 us -> 0.69 us
  other arithmetic: 9 us -> 2.21 us
  starting transfers between devices: 3.81 us -> 0 us
    reduce_scatter x2 -> x0, waiting for transfers between devices: 117 us -> none  [the longest x1 62.5 us: local(): small = lax.psum(lax.psum_scatter(small, 'dp', scatter_dimension=0), 'seq')]
    pallas_call x1, Pallas kernels: 17.9 us -> 50.9 us  [fused(): pl.pallas_call(functools.partial(fused_kernel, kernel_width), out_shape=(...]
    all_gather x1 -> x0, blocking collectives: 32.4 us -> none  [local(): packs = lax.all_gather(packed, 'dp', axis=0)]
    psum x1 -> x0, waiting for transfers between devices: 30.9 us -> none  [local(): lax.psum(lax.psum_scatter(gw, 'dp', scatter_dimension=0, tiled=True), 'seq')]
    psum x1 -> x0, blocking collectives: 11.2 us -> none  [local(): small = lax.psum(lax.psum_scatter(small, 'dp', scatter_dimension=0), 'seq')]
    another operation x5 -> x0, other arithmetic: 4.62 us -> none
    ppermute x2 -> x0, starting transfers between devices: 3.65 us -> none  [the longest x1 2.36 us: local(): before = lax.ppermute(codes[:, half - 128:], 'seq', up)]
  transfers between devices with their start and end apart: 6 -> 0, of which waited for: 4 -> 0; matrix products, arithmetic and copies ran while one was open for 5% -> 0% of each run, Pallas kernels for 0% -> 0%
where the time goes in v2:
time: 61.1 us; the launch traced here: 60.7 us
  Pallas kernels  50.9 us (83%)
  local copies, waits for them, and re-layouts  6.95 us (11%)
  other arithmetic  2.21 us (4%)
  between operations  0.69 us (1%)
    pallas_call x1, Pallas kernels, fused(): pl.pallas_call(functools.partial(fused_kernel, kernel_width), out_shape=(...  50.9 us
    unnamed x7, local copies, waits for them, and re-layouts  4.68 us

profile of v2, /device:TPU:0, one launch (start us, length us, event | category | flops | bytes accessed | tf_op | source)
XLA Modules:
  0.0 60.7 jit_solution(3082851198904078533)
XLA Ops:
  0.6 0.7 %add_reduce_fusion = s32[1536]{0:T(1024)S(1)} fusion(s32[1,1536]{1,0:T(1,128)} %param.7), kind=kLoop, calls=%fused_computation.6 | loop fusion | flops 1536 | bytes 12288 | tf_op jit(solution)/shard_map/add | solution.py:429
  1.3 0.3 add.20
  1.7 0.1 copy.15
  1.9 0.1 pad.29.clone
  1.9 0.7 %maximum_bitcast_fusion = bf16[4,1,96]{2,0,1:T(4,128)(2,1)S(1)} fusion(bf16[1,96]{1,0:T(2,128)(2,1)} %bitcast.29, bf16[1,96]{1,0:T(2,128)(2,1)} %bitcast.30, bf16[4]{0:T(256)(128)(2,1)S(1)} %pad.29.clone), kind=kLoop, calls=%fused_computation.7 | loop fusion | flops 2304 | bytes 1160 | tf_op jit(solution)/shard_map/broadcast_in_dim | solution.py:431
  2.7 0.7 %pad_maximum_fusion = bf16[4,16,96]{2,0,1:T(4,128)(2,1)S(1)} fusion(bf16[4,1,96]{2,0,1:T(4,128)(2,1)S(1)} %maximum_bitcast_fusion, bf16[4,15,96]{2,0,1:T(4,128)(2,1)} %bitcast.28), kind=kLoop, calls=%fused_computation.5 | loop fusion | flops 6144 | bytes 24576 | tf_op jit(solution)/shard_map/concatenate | solution.py:432
  3.4 0.7 %pad_bitcast_fusion = bf16[1,128]{1,0:T(2,128)(2,1)S(1)} fusion(bf16[112]{0:T(256)(128)(2,1)} %param.12), kind=kLoop, calls=%fused_computation.11 | loop fusion | bytes 480 | tf_op jit(solution)/shard_map/broadcast_in_dim | solution.py:434
  4.1 0.0 copy-start
  4.1 1.3 %copy-done = bf16[1,768,896]{2,1,0:T(8,128)(2,1)S(1)} copy-done((bf16[1,768,896]{2,1,0:T(8,128)(2,1)S(1)}, bf16[1,768,896]{2,1,0:T(8,128)(2,1)}, u32[]{:S(2)}) %copy-start) | copy-done | bytes 1376280
  5.5 0.0 copy-start.1
  5.5 0.9 %copy-done.1 = bf16[96,896]{1,0:T(8,128)(2,1)S(1)} copy-done((bf16[96,896]{1,0:T(8,128)(2,1)S(1)}, bf16[96,896]{1,0:T(8,128)(2,1)}, u32[]{:S(2)}) %copy-start.1) | copy-done | bytes 172056
  6.4 50.9 %fused_step.1 = (bf16[768,896]{1,0:T(8,128)(2,1)S(1)}, f32[96,896]{1,0:T(8,128)S(1)}, f32[128,128]{1,0:T(8,128)S(1)}) custom-call(s32[8,768]{1,0:T(8,128)S(1)} %pad.18.codes_ref, f32[128,128]{1,0:T(8,128)S(1)} %pad_convert_fusion.rows_ref, bf16[96,896]{1,0:T(8,128)(2,1)S(1)} %copy-done.1, bf16[768,896]{1,0:T(8,128)(2,1)S(1)} %bitcast.22), custom_call_target="tpu_custom_call" | custom-call | tf_op jit(solution)/shard_map/fused_step/pallas_call | solution.py:375
  57.3 0.5 slice_bitcast_fusion.1
  57.8 0.6 %copy.20 = f32[4,15,96]{2,0,1:T(4,128)} copy(f32[4,15,96]{2,1,0:T(8,128)S(1)} %bitcast.24) | data formatting | bytes 46080
  58.4 0.5 slice_bitcast_fusion
  58.9 1.1 %copy.23 = bf16[1,768,896]{2,1,0:T(8,128)(2,1)} copy(bf16[1,768,896]{2,1,0:T(8,128)(2,1)S(1)} %bitcast.23) | data formatting | bytes 2752512
  60.0 0.7 %copy.24 = f32[96,896]{1,0:T(8,128)} copy(f32[96,896]{1,0:T(8,128)S(1)} %get-tuple-element.24) | data formatting | bytes 688128
  (6 shorter events, 0.0 us)
Async XLA Ops:
  4.1 1.3 %copy-start = (bf16[1,768,896]{2,1,0:T(8,128)(2,1)S(1)}, bf16[1,768,896]{2,1,0:T(8,128)(2,1)}, u32[]{:S(2)}) copy-start(bf16[1,768,896]{2,1,0:T(8,128)(2,1)} %param.13) | copy-start | bytes 4128772
  5.5 0.9 %copy-start.1 = (bf16[96,896]{1,0:T(8,128)(2,1)S(1)}, bf16[96,896]{1,0:T(8,128)(2,1)}, u32[]{:S(2)}) copy-start(bf16[96,896]{1,0:T(8,128)(2,1)} %w_ref.1) | copy-start | bytes 516100

commit v3 on v0

--- a/solution.py
+++ b/solution.py
@@ -1,7 +1,456 @@
+import functools
+
 import jax
 import jax.numpy as jnp
 from jax import lax
+from jax.experimental import pallas as pl
+from jax.experimental.pallas import tpu as pltpu
 from jax.sharding import PartitionSpec as P
+
+F32, BF16 = jnp.float32, jnp.bfloat16
+CUBIC = 0.044715
+ROOT = 0.7978845608028654
+NN = (((1,), (0,)), ((), ()))
+NT = (((1,), (1,)), ((), ()))
+TN = (((0,), (0,)), ((), ()))
+MESH = pl.DeviceIdType.MESH
+STEP = 16
+
+
+def dot(a, b, dims):
+    return lax.dot_general(a, b, dims, preferred_element_type=F32)
+
+
+def build_features(bases_ref, halo_ref, stack_ref, wide_ref, feat_ref, kernel_width):
+    length = bases_ref.shape[1]
+    half, total = length // 2, length + 256
+    ext = jnp.concatenate([halo_ref[0:1], bases_ref[...] + 1, halo_ref[1:2]], axis=1)
+    ext = jnp.broadcast_to(ext, (8, total))
+    for k in range(kernel_width):
+        shift = k - kernel_width // 2
+        moved = ext if shift == 0 else pltpu.roll(ext, (-shift) % total, 1)
+        stack_ref[k : k + 1, :] = moved[0:1, 128 : 128 + length]
+    stack_ref[kernel_width : kernel_width + 1, :] = jnp.ones((1, length), jnp.int32)
+    stack = stack_ref[...]
+    hot = jnp.concatenate([jnp.where(stack == c + 1, 1.0, 0.0) for c in range(4)] * 2, axis=0)
+    wide_ref[...] = hot.T
+    for parity in range(2):
+        feat_ref[parity] = wide_ref[pl.ds(parity, half, stride=2), :][:, :64].astype(BF16)
+
+
+def forward_chunk(start, size, feat_ref, weight, gain, emb_ref, scaled_ref, slope_ref, inv_ref, pact_ref):
+    for parity in range(2):
+        emb_ref[parity] = dot(feat_ref[parity, pl.ds(start, size), :], weight, NT)
+    for r in range(0, size, STEP):
+        rows = pl.ds(start + r, STEP)
+        total = None
+        for parity in range(2):
+            emb = emb_ref[parity, r : r + STEP, :].astype(BF16).astype(F32)
+            inverse = lax.rsqrt(jnp.mean(emb * emb, axis=1, keepdims=True) + 1e-6)
+            scaled = emb * inverse
+            x = scaled * gain
+            sq = x * x
+            t = 0.5 + 0.5 * jnp.tanh(x * (ROOT + (ROOT * CUBIC) * sq))
+            act = x * t
+            slope = t + act * (1.0 - t) * (2.0 * ROOT + (6.0 * ROOT * CUBIC) * sq)
+            scaled_ref[parity, rows, :] = scaled
+            slope_ref[parity, rows, :] = slope
+            inv_ref[parity, rows, :] = jnp.broadcast_to(inverse, (STEP, 128))
+            total = act if total is None else total + act
+        pact_ref[rows, :] = total.astype(BF16)
+
+
+def backward_chunk(start, size, cot_ref, w, gain, ga_ref, scaled_ref, slope_ref, inv_ref, ge_ref, acc_ref):
+    ga_ref[...] = dot(cot_ref[start : start + size, :], w, NT)
+    width = ga_ref.shape[1]
+    acc = acc_ref[...]
+    for r in range(0, size, STEP):
+        rows = slice(start + r, start + r + STEP)
+        ga = ga_ref[r : r + STEP, :]
+        for parity in range(2):
+            scaled = scaled_ref[parity, rows, :]
+            inverse = inv_ref[parity, rows, 0:1]
+            u = ga * slope_ref[parity, rows, :]
+            q = u * scaled
+            acc = acc + (q[:8] + q[8:])
+            mean = jnp.sum(q * gain, axis=1, keepdims=True) * (1.0 / width)
+            ge = inverse * (u * gain - scaled * mean)
+            ge_ref[parity, rows, :] = ge.astype(BF16)
+    acc_ref[...] = acc
+
+
+def fused_kernel(
+    kernel_width,
+    bases_hbm, ew_hbm, eb_hbm, gain_hbm, w_hbm, pb_hbm, cot_hbm,
+    pooled_hbm, gw_ref, small_out,
+    pooled, bases, ew, eb, gain_in, pb, halo, stack, wide, feat, emb, scaled, slope, inv, pact, ge, ga, acc,
+    rows_in, pack, packs, wbuf, cot, gwb, s1buf, p1, s2buf, sum2, s3buf, fin, small, sbuf, tbuf,
+    send_sem, halo_recv, pack_recv, w_recv, s1_recv, s2_recv, s3_recv, fin_recv,
+    small_recv, t_recv, local_sem,
+):
+    dp, seq = 8, 4
+    length = bases.shape[1]
+    half = length // 2
+    part0, d1 = w_hbm.shape
+    d0, part1, part_h = part0 * dp, d1 // dp, part0 // 2
+    me, pos = lax.axis_index("dp"), lax.axis_index("seq")
+    z, y, x, c = me // 2, me % 2, pos // 2, pos % 2
+    y2, x2, c2 = 1 - y, 1 - x, 1 - c
+    mate, across, skew = 2 * x + c2, 2 * x2 + c, 2 * x2 + c2
+    own_rank = z % 2 == x
+    factor = 0.25 / (half * seq * dp)
+
+    barrier = pltpu.get_barrier_semaphore()
+    for j in range(1, dp):
+        pl.semaphore_signal(
+            barrier, inc=1, device_id={"dp": (me + j) % dp, "seq": pos}, device_id_type=MESH
+        )
+    for j in range(1, seq):
+        for to in (me, 2 * z + y2):
+            pl.semaphore_signal(
+                barrier, inc=1, device_id={"dp": to, "seq": (pos + j) % seq}, device_id_type=MESH
+            )
+
+    loads = [
+        pltpu.make_async_copy(src, dst, local_sem.at[i])
+        for i, (src, dst) in enumerate(
+            [
+                (ew_hbm, ew), (eb_hbm, eb), (gain_hbm, gain_in), (pb_hbm, pb), (bases_hbm, bases),
+                (w_hbm.at[:part_h], wbuf.at[me, 0]), (w_hbm.at[part_h:], wbuf.at[me, 1]),
+                (cot_hbm, cot),
+            ]
+        )
+    ]
+    for load in loads:
+        load.start()
+    rows_in[...] = jnp.zeros_like(rows_in)
+    acc[...] = jnp.zeros_like(acc)
+    for load in loads[:4]:
+        load.wait()
+    values = ew[...].astype(F32)
+    for letter in range(4):
+        rows_in[16 * letter : 16 * letter + kernel_width, :part0] = values[:, letter, :]
+    rows_in[15:16, :part0] = eb[...].astype(F32)
+    rows_in[31:32, :part0] = gain_in[...].astype(F32)
+    turned = rows_in[...].T
+    pack[:part_h, :] = jnp.concatenate(
+        [turned[:part_h, :64], turned[part_h:part0, :64]], axis=1
+    ).astype(BF16)
+    tail = jnp.concatenate([pb[...].astype(F32), jnp.zeros((1, 128 - part1), F32)], axis=1)
+    pack[part_h:, :] = jnp.broadcast_to(tail, (16, 128)).astype(BF16)
+    packs[me] = pack[...]
+    for load in loads[4:7]:
+        load.wait()
+
+    pl.semaphore_wait(barrier, dp - 1 + 2 * (seq - 1))
+
+    started = []
+
+    def send(src, dst, recv, to_dp, to_seq, pred=None):
+        copy = pltpu.make_async_remote_copy(
+            src_ref=src, dst_ref=dst, send_sem=send_sem.at[len(started)], recv_sem=recv,
+            device_id={"dp": to_dp, "seq": to_seq}, device_id_type=MESH,
+        )
+        started.append((copy, pred))
+        if pred is None:
+            copy.start()
+        else:
+            pl.when(pred)(lambda: copy.start())
+
+    def arrive(dst, recv, pred=None):
+        copy = pltpu.make_async_remote_copy(
+            src_ref=dst, dst_ref=dst, send_sem=send_sem.at[0], recv_sem=recv,
+            device_id={"dp": me, "seq": mate}, device_id_type=MESH,
+        )
+        if pred is None:
+            copy.wait_recv()
+        else:
+            pl.when(pred)(lambda: copy.wait_recv())
+
+    send(bases.at[:, length - 128 :], halo.at[0:1], halo_recv.at[0], me, pos + 1, pos < seq - 1)
+    send(bases.at[:, :128], halo.at[1:2], halo_recv.at[1], me, pos - 1, pos > 0)
+    for j in range(1, dp):
+        send(pack, packs.at[me], pack_recv.at[me], (me + j) % dp, pos)
+    for zz in range(4):
+        send(wbuf.at[me, c], wbuf.at[me, c], w_recv.at[me, c], 2 * zz + y, pos,
+             own_rank & (z != zz))
+    send(wbuf.at[me, c], wbuf.at[me, c], w_recv.at[me, c], 2 * z + y2, pos)
+
+    arrive(halo.at[0:1], halo_recv.at[0], pos > 0)
+    arrive(halo.at[1:2], halo_recv.at[1], pos < seq - 1)
+    for side, edge in ((0, 0), (1, seq - 1)):
+
+        @pl.when(pos == edge)
+        def _(side=side):
+            halo[side : side + 1, :] = jnp.zeros((1, 128), jnp.int32)
+
+        @pl.when(pos != edge)
+        def _(side=side):
+            halo[side : side + 1, :] = halo[side : side + 1, :] + 1
+
+
+    build_features(bases, halo, stack, wide, feat, kernel_width)
+    for j in range(1, dp):
+        arrive(packs.at[(me + j) % dp], pack_recv.at[(me + j) % dp])
+    weight = jnp.concatenate(
+        [packs[d, :part_h, 64 * h : 64 * h + 64] for d in range(dp) for h in range(2)], axis=0
+    )
+    lanes = lax.broadcasted_iota(jnp.int32, (16, 64), 1)
+    gain = dot(jnp.where(lanes == 31, 1.0, 0.0).astype(BF16), weight, NT)[0:1]
+    size = 128
+    chunks = half // size
+
+    def forward(first, last):
+        @pl.loop(first, last)
+        def _(i):
+            start = pl.multiple_of(i * size, size)
+            forward_chunk(start, size, feat, weight, gain, emb, scaled, slope, inv, pact)
+
+    forward(0, chunks // 3)
+    for zz in range(4):
+        d = 2 * zz + y
+        slot, sem = wbuf.at[d, c], w_recv.at[d, c]
+        direct = (z != zz) & (x == zz % 2)
+        arrive(slot, sem, direct)
+        send(slot, slot, sem, 2 * z + y2, across, direct)
+        send(slot, slot, sem, 2 * z + y2, pos, direct)
+        send(slot, slot, sem, me, across, direct)
+        send(slot, slot, sem, me, mate, direct)
+    d = 2 * z + y2
+    arrive(wbuf.at[d, c], w_recv.at[d, c])
+    send(wbuf.at[d, c], wbuf.at[d, c], w_recv.at[d, c], me, mate)
+    forward(chunks // 3, chunks)
+
+    loads[7].wait()
+    block = d0 // 2
+    for b in range(2):
+        value = dot(pact[:, b * block : (b + 1) * block], cot[...], TN)
+        gwb[4 * b : 4 * b + 4] = value.astype(BF16).reshape(4, 2, part_h, d1)
+        send(gwb.at[4 * b : 4 * b + 4, c2], s1buf.at[b], s1_recv.at[b], me, mate)
+
+    for zz in range(4):
+        d = 2 * zz + y
+        slot, sem = wbuf.at[d, c], w_recv.at[d, c]
+        relayed = (z != zz) & (x != zz % 2)
+        arrive(slot, sem, relayed)
+        send(slot, slot, sem, me, mate, relayed)
+        d = 2 * zz + y2
+        slot, sem = wbuf.at[d, c], w_recv.at[d, c]
+        arrive(slot, sem, z != zz)
+        send(slot, slot, sem, me, mate, z != zz)
+
+    rank = 2 * x + y
+    others = (
+        (2 * x2 + y2, 2 * z + y2, across),
+        (2 * x + y2, 2 * z + y2, pos),
+        (2 * x2 + y, me, across),
+    )
+    for b in range(2):
+        arrive(s1buf.at[b], s1_recv.at[b])
+        for k in range(4):
+            p1[b, k] = (gwb[4 * b + k, c].astype(F32) + s1buf[b, k].astype(F32)).astype(BF16)
+        for piece, to_dp, to_seq in others:
+            send(p1.at[b, piece], s2buf.at[b, rank], s2_recv.at[b, rank], to_dp, to_seq)
+
+    for d in range(dp):
+        arrive(wbuf.at[d, c2], w_recv.at[d, c2], me != d)
+
+    tails = jnp.concatenate([packs[d, part_h:, :][0:1].astype(F32) for d in range(dp)], axis=0)
+    tails = jnp.concatenate([tails, jnp.zeros((8, 128), F32)], axis=0).astype(BF16)
+    columns = lax.broadcasted_iota(jnp.int32, (128, d1), 1)
+    lane = lax.broadcasted_iota(jnp.int32, (128, d1), 0)
+    place = jnp.where((columns % part1) == lane, 1.0, 0.0).astype(BF16)
+    spread = dot(tails, place, NN)
+    holder = lax.broadcasted_iota(jnp.int32, (16, d1), 0)
+    column = lax.broadcasted_iota(jnp.int32, (16, d1), 1)
+    bias = jnp.sum(jnp.where(column // part1 == holder, spread, 0.0), axis=0, keepdims=True)
+
+    big = half // 3
+    for i in range(3):
+        w = wbuf[...].reshape(d0, d1)
+        value = 0.5 * dot(pact[i * big : (i + 1) * big, :], w, NN) + bias
+        pooled[i * big : (i + 1) * big, :] = value.astype(BF16)
+    pooled_out = pltpu.make_async_copy(pooled, pooled_hbm, local_sem.at[8])
+    pooled_out.start()
+
+    def backward(i):
+        w = wbuf[...].reshape(d0, d1)
+        backward_chunk(i * big, big, cot, w, gain, ga.at[i % 2], scaled, slope, inv, ge, acc)
+
+    def plane_sum(k):
+        total = p1[k, rank].astype(F32)
+        for piece, _, _ in others:
+            arrive(s2buf.at[k, piece], s2_recv.at[k, piece])
+            total = total + s2buf[k, piece].astype(F32)
+        sum2[k] = total.astype(BF16)
+        zt = x + 2 * k
+        send(sum2.at[k], s3buf.at[z], s3_recv.at[z], 2 * zt + y, pos, zt != z)
+
+    backward(0)
+    plane_sum(0)
+    backward(1)
+    plane_sum(1)
+    backward(2)
+
+    g = dot(feat[0], ge[0], TN) + dot(feat[1], ge[1], TN)
+    gain_row = jnp.sum(acc[...], axis=0, keepdims=True)
+    g = jnp.where(lax.broadcasted_iota(jnp.int32, (64, d0), 0) == 31, gain_row, g)
+    turned = jnp.concatenate([g, jnp.zeros_like(g)], axis=0).T
+    for d in range(dp):
+        low = turned[d * part0 : d * part0 + part_h, :64]
+        high = turned[d * part0 + part_h : (d + 1) * part0, :64]
+        small[d, :part_h, :] = jnp.concatenate([low, high], axis=1).astype(BF16)
+    sums = 2.0 * dot(jnp.ones((16, half), BF16), cot[...], NN)[0:8]
+    for d in range(dp):
+        own = jnp.concatenate(
+            [sums[:, d * part1 : (d + 1) * part1], jnp.zeros((8, 128 - part1), F32)], axis=1
+        )
+        small[d, part_h:, :] = jnp.concatenate([own, own], axis=0).astype(BF16)
+    for j in range(1, dp):
+        to = (me + j) % dp
+        send(small.at[to], sbuf.at[me], small_recv.at[me], to, pos)
+    sbuf[me] = small[me]
+
+    for zz in range(4):
+        arrive(s3buf.at[zz], s3_recv.at[zz], own_rank & (z != zz))
+
+    @pl.when(own_rank)
+    def _():
+        value = sum2[z // 2].astype(F32)
+        for j in range(1, 4):
+            value = value + s3buf[(z + j) % 4].astype(F32)
+        fin[c] = value.astype(BF16)
+
+    send(fin.at[c], fin.at[c], fin_recv.at[c], me, across, own_rank)
+    arrive(fin.at[c], fin_recv.at[c], jnp.logical_not(own_rank))
+    send(fin.at[c], fin.at[c], fin_recv.at[c], me, mate)
+
+    for j in range(1, dp):
+        arrive(sbuf.at[(me + j) % dp], small_recv.at[(me + j) % dp])
+    tbuf[pos] = jnp.sum(sbuf[...].astype(F32), axis=0).astype(BF16)
+    for j in range(1, seq):
+        send(tbuf.at[pos], tbuf.at[pos], t_recv.at[pos], me, (pos + j) % seq)
+
+    arrive(fin.at[c2], fin_recv.at[c2])
+    gw_ref[...] = fin[...].astype(F32).reshape(part0, d1) * factor
+    for j in range(1, seq):
+        arrive(tbuf.at[(pos + j) % seq], t_recv.at[(pos + j) % seq])
+    small_out[...] = jnp.sum(tbuf[...].astype(F32), axis=0) * factor
+
+    for copy, pred in started:
+        if pred is None:
+            copy.wait_send()
+        else:
+            pl.when(pred)(lambda copy=copy: copy.wait_send())
+    pooled_out.wait()
+
+
+def finish_kernel(kernel_width, pooled_in, gw_in, small, pooled, gew, geb, ggain, gw, gpb, turned, sems):
+    part0, part1 = gw_in.shape[0], gpb.shape[1]
+    part_h = part0 // 2
+    copies = [
+        pltpu.make_async_copy(pooled_in, pooled, sems.at[0]),
+        pltpu.make_async_copy(gw_in, gw, sems.at[1]),
+    ]
+    for copy in copies:
+        copy.start()
+    gpb[...] = small[part_h : part_h + 1, :part1]
+    low, high = small[:part_h, :64], small[:part_h, 64:]
+    channels = jnp.concatenate([low, high, jnp.zeros((128 - part0, 64), F32)], axis=0)
+    turned[...] = jnp.concatenate([channels, channels], axis=1).T
+    for letter in range(4):
+        gew[:, letter, :] = turned[16 * letter : 16 * letter + kernel_width, :part0]
+    geb[...] = turned[15:16, :part0]
+    ggain[...] = turned[31:32, :part0]
+    for copy in copies:
+        copy.wait()
+
+
+def shape(dims, kind):
+    return jax.ShapeDtypeStruct(dims, kind)
+
+
+def fused(bases, embed_weight, embed_bias, norm_gain, proj_weight, proj_bias, cotangent):
+    kernel_width = embed_weight.shape[0]
+    length = bases.shape[1]
+    half = length // 2
+    part0, d1 = proj_weight.shape
+    part1 = proj_bias.shape[0]
+    dp, seq = 8, 4
+    d0, part_h = part0 * dp, part0 // 2
+    big = half // 3
+    vmem, hbm = pl.BlockSpec(memory_space=pltpu.VMEM), pl.BlockSpec(memory_space=pl.ANY)
+    dma = pltpu.SemaphoreType.DMA
+    scratch = [
+        ((half, d1), BF16),
+        ((1, length), jnp.int32),
+        (embed_weight.shape, BF16),
+        ((1, part0), BF16),
+        ((1, part0), BF16),
+        ((1, part1), BF16),
+        ((2, 128), jnp.int32),
+        ((16, length), jnp.int32),
+        ((length, 128), F32),
+        ((2, half, 64), BF16),
+        ((2, 128, d0), F32),
+        ((2, half, d0), F32),
+        ((2, half, d0), F32),
+        ((2, half, 128), F32),
+        ((half, d0), BF16),
+        ((2, half, d0), BF16),
+        ((2, big, d0), F32),
+        ((8, d0), F32),
+        ((128, 128), F32),
+        ((part_h + 16, 128), BF16),
+        ((dp, part_h + 16, 128), BF16),
+        ((dp, 2, part_h, d1), BF16),
+        ((half, d1), BF16),
+        ((dp, 2, part_h, d1), BF16),
+        ((2, 4, part_h, d1), BF16),
+        ((2, 4, part_h, d1), BF16),
+        ((2, 4, part_h, d1), BF16),
+        ((2, part_h, d1), BF16),
+        ((4, part_h, d1), BF16),
+        ((2, part_h, d1), BF16),
+        ((dp, part_h + 16, 128), BF16),
+        ((dp, part_h + 16, 128), BF16),
+        ((seq, part_h + 16, 128), BF16),
+    ]
+    pooled, gw, small = pl.pallas_call(
+        functools.partial(fused_kernel, kernel_width),
+        out_shape=(
+            shape((half, d1), BF16), shape((part0, d1), F32), shape((part_h + 16, 128), F32)
+        ),
+        in_specs=[hbm] * 7,
+        out_specs=(hbm, vmem, vmem),
+        scratch_shapes=[pltpu.VMEM(dims, kind) for dims, kind in scratch]
+        + [dma((n,)) for n in (72, 2, dp)]
+        + [dma((dp, 2)), dma((2,)), dma((2, 4)), dma((4,)), dma((2,)), dma((dp,)), dma((seq,)), dma((9,))],
+        compiler_params=pltpu.CompilerParams(
+            collective_id=0, has_side_effects=True, vmem_limit_bytes=60 * 2**20
+        ),
+        name="fused_step",
+    )(
+        bases, embed_weight, embed_bias[None], norm_gain[None], proj_weight, proj_bias[None],
+        cotangent[0],
+    )
+    outs = pl.pallas_call(
+        functools.partial(finish_kernel, kernel_width),
+        out_shape=(
+            shape((half, d1), BF16),
+            shape(embed_weight.shape, F32),
+            shape((1, part0), F32),
+            shape((1, part0), F32),
+            shape((part0, d1), F32),
+            shape((1, part1), F32),
+        ),
+        in_specs=[pl.BlockSpec(memory_space=pl.ANY), pl.BlockSpec(memory_space=pl.ANY), vmem],
+        out_specs=(hbm, vmem, vmem, vmem, hbm, vmem),
+        scratch_shapes=[pltpu.VMEM((128, 128), F32), dma((2,))],
+        compiler_params=pltpu.CompilerParams(vmem_limit_bytes=60 * 2**20),
+        name="finish_step",
+    )(pooled, gw, small)
+    return (outs[0][None], outs[1], outs[2][0], outs[3][0], outs[4], outs[5][0])
 
 
 def with_halo(x, sides, width):
@@ -17,7 +466,7 @@
     return x
 
 
-def local(bases, embed_weight, embed_bias, norm_gain, proj_weight, proj_bias, cotangent):
+def plain(bases, embed_weight, embed_bias, norm_gain, proj_weight, proj_bias, cotangent):
     kernel_width = embed_weight.shape[0]
     row_count = bases.shape[1]
     codes = bases + 1
@@ -96,8 +545,9 @@
         P("dp"),
         P("dp", "seq", None),
     )
+    step = fused if (mesh.shape["dp"], mesh.shape["seq"]) == (8, 4) else plain
     return jax.shard_map(
-        local,
+        step,
         mesh=mesh,
         in_specs=placed,
         out_specs=(

time: 292 us -> 98.3 us (0.34)
  blocking collectives: 103 us -> 0 us
  Pallas kernels: 0 us -> 97.4 us
  waiting for transfers between devices: 70.4 us -> 0 us
  local copies, waits for them, and re-layouts: 46.7 us -> 0 us
  other arithmetic: 24.7 us -> 0 us
  matrix products: 24.3 us -> 0 us
  between operations: 16.6 us -> 0.64 us
  starting transfers between devices: 5.46 us -> 0 us
    pallas_call x0 -> x2, Pallas kernels: none -> 97.4 us  [the longest x1 54.6 us: fused(): pl.pallas_call(functools.partial(finish_kernel, kernel_width), out_shape=...]
    unnamed x2 -> x0, blocking collectives: 59.4 us -> none
    all_gather x1 -> x0, blocking collectives: 32.4 us -> none  [local(): lax.all_gather(embed_weight, 'dp', axis=2, tiled=True)]
    unnamed x5 -> x0, waiting for transfers between devices: 27.7 us -> none
    dot_general x5 -> x0, matrix products: 24.3 us -> none  [the longest x1 8.43 us: local(): lax.dot_general(grad_mixed, full_proj, (((1,), (1,)), ((), ())), preferre...]
    reduce_scatter x1 -> x0, waiting for transfers between devices: 21.7 us -> none  [local(): lax.psum_scatter(whole[3], 'dp', scatter_dimension=0, tiled=True)]
    psum x1 -> x0, waiting for transfers between devices: 21 us -> none  [local(): lax.psum((grad_embed_weight, grad_embed_bias, grad_norm_gain, grad_proj_w...]
    unnamed x34 -> x0, local copies, waits for them, and re-layouts: 18.4 us -> none
  transfers between devices with their start and end apart: 6 -> 0, of which waited for: 3 -> 0; matrix products, arithmetic and copies ran while one was open for 32% -> 0% of each run, Pallas kernels for 0% -> 0%
where the time goes in v3:
time: 98.3 us; the launch traced here: 98 us
  Pallas kernels  97.4 us (99%)
    pallas_call x1, Pallas kernels, fused(): pl.pallas_call(functools.partial(finish_kernel, kernel_width), out_shape=...  54.6 us
    pallas_call x1, Pallas kernels, fused(): pl.pallas_call(functools.partial(fused_kernel, kernel_width), out_shape=(...  42.8 us

profile of v3, /device:TPU:0, one launch (start us, length us, event | category | flops | bytes accessed | tf_op | source)
XLA Modules:
  0.0 98.0 jit_solution(14264301586351224067)
XLA Ops:
  0.6 42.8 %fused_step.1 = (bf16[768,896]{1,0:T(8,128)(2,1)}, f32[96,896]{1,0:T(8,128)}, f32[64,128]{1,0:T(8,128)}) custom-call(s32[1,1536]{1,0:T(1,128)} %bases_hbm.1, bf16[15,4,96]{2,1,0:T(4,128)(2,1)} %ew_hbm.1, bf16[1,96]{1,0:T(2,128)(2,1)} %bitcast.9, bf16[1,96]{1,0:T(2,128)(2,1)} %bitcast.10, bf16[96,896]{1,0:T(8,128)(2,1)} %w_hbm.1, bf16[1,112]{1,0:T(2,128)(2,1)} %bitcast.11, ...), custom_call_target="tpu_custom_call" | custom-call | tf_op jit(solution)/shard_map/fused_step/pallas_call | solution.py:419
  43.4 54.6 %finish_step.1 = (bf16[768,896]{1,0:T(8,128)(2,1)}, f32[15,4,96]{2,1,0:T(4,128)}, f32[1,96]{1,0:T(1,128)}, f32[1,96]{1,0:T(1,128)}, f32[96,896]{1,0:T(8,128)}, /*index=5*/f32[1,112]{1,0:T(1,128)}) custom-call(bf16[768,896]{1,0:T(8,128)(2,1)} %get-tuple-element.15.pooled_in, f32[96,896]{1,0:T(8,128)} %get-tuple-element.16.gw_in, ...), custom_call_target="tpu_custom_call" | custom-call | tf_op jit(solution)/shard_map/finish_step/pallas_call | solution.py:437

commit v4 on v3

--- a/solution.py
+++ b/solution.py
@@ -15,6 +15,7 @@
 TN = (((0,), (0,)), ((), ()))
 MESH = pl.DeviceIdType.MESH
 STEP = 16
+PIECES = 4
 
 
 def dot(a, b, dims):
@@ -172,8 +173,7 @@
     for j in range(1, dp):
         send(pack, packs.at[me], pack_recv.at[me], (me + j) % dp, pos)
     for zz in range(4):
-        send(wbuf.at[me, c], wbuf.at[me, c], w_recv.at[me, c], 2 * zz + y, pos,
-             own_rank & (z != zz))
+        send(wbuf.at[me, c], wbuf.at[me, c], w_recv.at[me, c], 2 * zz + y, pos, z != zz)
     send(wbuf.at[me, c], wbuf.at[me, c], w_recv.at[me, c], 2 * z + y2, pos)
 
     arrive(halo.at[0:1], halo_recv.at[0], pos > 0)
@@ -206,20 +206,24 @@
             start = pl.multiple_of(i * size, size)
             forward_chunk(start, size, feat, weight, gain, emb, scaled, slope, inv, pact)
 
+    def relay(distances):
+        for zz in range(4):
+            d = 2 * zz + y
+            slot, sem = wbuf.at[d, c], w_recv.at[d, c]
+            for distance in distances:
+                there = (z == zz - distance) | (z == zz + distance)
+                arrive(slot, sem, there)
+                send(slot, slot, sem, 2 * z + y2, pos, there)
+                send(slot, slot, sem, me, mate, there)
+
     forward(0, chunks // 3)
-    for zz in range(4):
-        d = 2 * zz + y
-        slot, sem = wbuf.at[d, c], w_recv.at[d, c]
-        direct = (z != zz) & (x == zz % 2)
-        arrive(slot, sem, direct)
-        send(slot, slot, sem, 2 * z + y2, across, direct)
-        send(slot, slot, sem, 2 * z + y2, pos, direct)
-        send(slot, slot, sem, me, across, direct)
-        send(slot, slot, sem, me, mate, direct)
+    relay((1,))
     d = 2 * z + y2
     arrive(wbuf.at[d, c], w_recv.at[d, c])
     send(wbuf.at[d, c], wbuf.at[d, c], w_recv.at[d, c], me, mate)
-    forward(chunks // 3, chunks)
+    forward(chunks // 3, 2 * chunks // 3)
+    relay((2, 3))
+    forward(2 * chunks // 3, chunks)
 
     loads[7].wait()
     block = d0 // 2
@@ -229,11 +233,6 @@
         send(gwb.at[4 * b : 4 * b + 4, c2], s1buf.at[b], s1_recv.at[b], me, mate)
 
     for zz in range(4):
-        d = 2 * zz + y
-        slot, sem = wbuf.at[d, c], w_recv.at[d, c]
-        relayed = (z != zz) & (x != zz % 2)
-        arrive(slot, sem, relayed)
-        send(slot, slot, sem, me, mate, relayed)
         d = 2 * zz + y2
         slot, sem = wbuf.at[d, c], w_recv.at[d, c]
         arrive(slot, sem, z != zz)
@@ -255,15 +254,8 @@
     for d in range(dp):
         arrive(wbuf.at[d, c2], w_recv.at[d, c2], me != d)
 
-    tails = jnp.concatenate([packs[d, part_h:, :][0:1].astype(F32) for d in range(dp)], axis=0)
-    tails = jnp.concatenate([tails, jnp.zeros((8, 128), F32)], axis=0).astype(BF16)
-    columns = lax.broadcasted_iota(jnp.int32, (128, d1), 1)
-    lane = lax.broadcasted_iota(jnp.int32, (128, d1), 0)
-    place = jnp.where((columns % part1) == lane, 1.0, 0.0).astype(BF16)
-    spread = dot(tails, place, NN)
-    holder = lax.broadcasted_iota(jnp.int32, (16, d1), 0)
-    column = lax.broadcasted_iota(jnp.int32, (16, d1), 1)
-    bias = jnp.sum(jnp.where(column // part1 == holder, spread, 0.0), axis=0, keepdims=True)
+    tails = [packs[d, part_h:, :].astype(F32)[:8, :part1] for d in range(dp)]
+    bias = jnp.concatenate(tails, axis=1)[0:1]
 
     big = half // 3
     for i in range(3):
@@ -287,10 +279,10 @@
         send(sum2.at[k], s3buf.at[z], s3_recv.at[z], 2 * zt + y, pos, zt != z)
 
     backward(0)
+    backward(1)
     plane_sum(0)
-    backward(1)
+    backward(2)
     plane_sum(1)
-    backward(2)
 
     g = dot(feat[0], ge[0], TN) + dot(feat[1], ge[1], TN)
     gain_row = jnp.sum(acc[...], axis=0, keepdims=True)
@@ -345,15 +337,21 @@
     pooled_out.wait()
 
 
-def finish_kernel(kernel_width, pooled_in, gw_in, small, pooled, gew, geb, ggain, gw, gpb, turned, sems):
+def finish_kernel(kernel_width, pooled_in, gw_in, small, pooled, gew, geb, ggain, gw, gpb, turned, held, held_gw, sems):
     part0, part1 = gw_in.shape[0], gpb.shape[1]
     part_h = part0 // 2
-    copies = [
-        pltpu.make_async_copy(pooled_in, pooled, sems.at[0]),
-        pltpu.make_async_copy(gw_in, gw, sems.at[1]),
-    ]
-    for copy in copies:
-        copy.start()
+    rows = pooled_in.shape[0] // PIECES
+    pieces = [
+        (pooled_in.at[pl.ds(i * rows, rows)], held.at[pl.ds(i * rows, rows)], pooled.at[pl.ds(i * rows, rows)])
+        for i in range(PIECES)
+    ] + [(gw_in, held_gw, gw)]
+    loads = [pltpu.make_async_copy(src, mid, sems.at[0, i]) for i, (src, mid, _) in enumerate(pieces)]
+    stores = [pltpu.make_async_copy(mid, dst, sems.at[1, i]) for i, (_, mid, dst) in enumerate(pieces)]
+    for load in loads:
+        load.start()
+    for load, store in zip(loads, stores):
+        load.wait()
+        store.start()
     gpb[...] = small[part_h : part_h + 1, :part1]
     low, high = small[:part_h, :64], small[:part_h, 64:]
     channels = jnp.concatenate([low, high, jnp.zeros((128 - part0, 64), F32)], axis=0)
@@ -362,8 +360,8 @@
         gew[:, letter, :] = turned[16 * letter : 16 * letter + kernel_width, :part0]
     geb[...] = turned[15:16, :part0]
     ggain[...] = turned[31:32, :part0]
-    for copy in copies:
-        copy.wait()
+    for store in stores:
+        store.wait()
 
 
 def shape(dims, kind):
@@ -446,7 +444,12 @@
         ),
         in_specs=[pl.BlockSpec(memory_space=pl.ANY), pl.BlockSpec(memory_space=pl.ANY), vmem],
         out_specs=(hbm, vmem, vmem, vmem, hbm, vmem),
-        scratch_shapes=[pltpu.VMEM((128, 128), F32), dma((2,))],
+        scratch_shapes=[
+            pltpu.VMEM((128, 128), F32),
+            pltpu.VMEM((half, d1), BF16),
+            pltpu.VMEM((part0, d1), F32),
+            dma((2, PIECES + 1)),
+        ],
         compiler_params=pltpu.CompilerParams(vmem_limit_bytes=60 * 2**20),
         name="finish_step",
     )(pooled, gw, small)

time: 98.3 us -> 50 us (0.51)
  Pallas kernels: 97.4 us -> 49.2 us
    pallas_call x1, Pallas kernels: 54.6 us -> 3.63 us  [fused(): pl.pallas_call(functools.partial(finish_kernel, kernel_width), out_shape=...]
    pallas_call x1, Pallas kernels: 42.8 us -> 45.5 us  [fused(): pl.pallas_call(functools.partial(fused_kernel, kernel_width), out_shape=(...]
where the time goes in v4:
time: 50 us; the launch traced here: 49.8 us
  Pallas kernels  49.2 us (98%)
  between operations  0.64 us (1%)
    pallas_call x1, Pallas kernels, fused(): pl.pallas_call(functools.partial(fused_kernel, kernel_width), out_shape=(...  45.5 us
    pallas_call x1, Pallas kernels, fused(): pl.pallas_call(functools.partial(finish_kernel, kernel_width), out_shape=...  3.63 us

profile of v4, /device:TPU:0, one launch (start us, length us, event | category | flops | bytes accessed | tf_op | source)
XLA Modules:
  0.0 49.8 jit_solution(623569278502959369)
XLA Ops:
  0.6 45.5 %fused_step.1 = (bf16[768,896]{1,0:T(8,128)(2,1)}, f32[96,896]{1,0:T(8,128)}, f32[64,128]{1,0:T(8,128)}) custom-call(s32[1,1536]{1,0:T(1,128)} %bases_hbm.1, bf16[15,4,96]{2,1,0:T(4,128)(2,1)} %ew_hbm.1, bf16[1,96]{1,0:T(2,128)(2,1)} %bitcast.9, bf16[1,96]{1,0:T(2,128)(2,1)} %bitcast.10, bf16[96,896]{1,0:T(8,128)(2,1)} %w_hbm.1, bf16[1,112]{1,0:T(2,128)(2,1)} %bitcast.11, ...), custom_call_target="tpu_custom_call" | custom-call | tf_op jit(solution)/shard_map/fused_step/pallas_call | solution.py:417
  46.2 3.6 %finish_step.1 = (bf16[768,896]{1,0:T(8,128)(2,1)}, f32[15,4,96]{2,1,0:T(4,128)}, f32[1,96]{1,0:T(1,128)}, f32[1,96]{1,0:T(1,128)}, f32[96,896]{1,0:T(8,128)}, /*index=5*/f32[1,112]{1,0:T(1,128)}) custom-call(bf16[768,896]{1,0:T(8,128)(2,1)} %get-tuple-element.15.pooled_in, f32[96,896]{1,0:T(8,128)} %get-tuple-element.16.gw_in, ...), custom_call_target="tpu_custom_call" | custom-call | tf_op jit(solution)/shard_map/finish_step/pallas_call | solution.py:435

commit v5 on v4

--- a/solution.py
+++ b/solution.py
@@ -172,9 +172,15 @@
     send(bases.at[:, :128], halo.at[1:2], halo_recv.at[1], me, pos - 1, pos > 0)
     for j in range(1, dp):
         send(pack, packs.at[me], pack_recv.at[me], (me + j) % dp, pos)
-    for zz in range(4):
-        send(wbuf.at[me, c], wbuf.at[me, c], w_recv.at[me, c], 2 * zz + y, pos, z != zz)
     send(wbuf.at[me, c], wbuf.at[me, c], w_recv.at[me, c], 2 * z + y2, pos)
+
+    def shard_out(distances):
+        for zz in range(4):
+            for distance in distances:
+                there = (z == zz - distance) | (z == zz + distance)
+                send(wbuf.at[me, c], wbuf.at[me, c], w_recv.at[me, c], 2 * zz + y, pos, there)
+
+    shard_out((1,))
 
     arrive(halo.at[0:1], halo_recv.at[0], pos > 0)
     arrive(halo.at[1:2], halo_recv.at[1], pos < seq - 1)
@@ -192,12 +198,13 @@
     build_features(bases, halo, stack, wide, feat, kernel_width)
     for j in range(1, dp):
         arrive(packs.at[(me + j) % dp], pack_recv.at[(me + j) % dp])
+    shard_out((3, 2))
     weight = jnp.concatenate(
         [packs[d, :part_h, 64 * h : 64 * h + 64] for d in range(dp) for h in range(2)], axis=0
     )
     lanes = lax.broadcasted_iota(jnp.int32, (16, 64), 1)
     gain = dot(jnp.where(lanes == 31, 1.0, 0.0).astype(BF16), weight, NT)[0:1]
-    size = 128
+    size = 256
     chunks = half // size
 
     def forward(first, last):
@@ -221,9 +228,7 @@
     d = 2 * z + y2
     arrive(wbuf.at[d, c], w_recv.at[d, c])
     send(wbuf.at[d, c], wbuf.at[d, c], w_recv.at[d, c], me, mate)
-    forward(chunks // 3, 2 * chunks // 3)
-    relay((2, 3))
-    forward(2 * chunks // 3, chunks)
+    forward(chunks // 3, chunks)
 
     loads[7].wait()
     block = d0 // 2
@@ -231,12 +236,8 @@
         value = dot(pact[:, b * block : (b + 1) * block], cot[...], TN)
         gwb[4 * b : 4 * b + 4] = value.astype(BF16).reshape(4, 2, part_h, d1)
         send(gwb.at[4 * b : 4 * b + 4, c2], s1buf.at[b], s1_recv.at[b], me, mate)
-
-    for zz in range(4):
-        d = 2 * zz + y2
-        slot, sem = wbuf.at[d, c], w_recv.at[d, c]
-        arrive(slot, sem, z != zz)
-        send(slot, slot, sem, me, mate, z != zz)
+        if b == 0:
+            relay((2, 3))
 
     rank = 2 * x + y
     others = (
@@ -250,6 +251,12 @@
             p1[b, k] = (gwb[4 * b + k, c].astype(F32) + s1buf[b, k].astype(F32)).astype(BF16)
         for piece, to_dp, to_seq in others:
             send(p1.at[b, piece], s2buf.at[b, rank], s2_recv.at[b, rank], to_dp, to_seq)
+
+    for zz in range(4):
+        d = 2 * zz + y2
+        slot, sem = wbuf.at[d, c], w_recv.at[d, c]
+        arrive(slot, sem, z != zz)
+        send(slot, slot, sem, me, mate, z != zz)
 
     for d in range(dp):
         arrive(wbuf.at[d, c2], w_recv.at[d, c2], me != d)
@@ -282,7 +289,6 @@
     backward(1)
     plane_sum(0)
     backward(2)
-    plane_sum(1)
 
     g = dot(feat[0], ge[0], TN) + dot(feat[1], ge[1], TN)
     gain_row = jnp.sum(acc[...], axis=0, keepdims=True)
@@ -302,6 +308,7 @@
         to = (me + j) % dp
         send(small.at[to], sbuf.at[me], small_recv.at[me], to, pos)
     sbuf[me] = small[me]
+    plane_sum(1)
 
     for zz in range(4):
         arrive(s3buf.at[zz], s3_recv.at[zz], own_rank & (z != zz))
@@ -337,31 +344,47 @@
     pooled_out.wait()
 
 
-def finish_kernel(kernel_width, pooled_in, gw_in, small, pooled, gew, geb, ggain, gw, gpb, turned, held, held_gw, sems):
+def finish_kernel(
+    kernel_width, pooled_in, gw_in, small_in, pooled, gew, geb, ggain, gw, gpb,
+    turned, held, held_gw, small, out_ew, out_eb, out_gain, out_pb, load_sem, store_sem,
+):
     part0, part1 = gw_in.shape[0], gpb.shape[1]
     part_h = part0 // 2
     rows = pooled_in.shape[0] // PIECES
-    pieces = [
-        (pooled_in.at[pl.ds(i * rows, rows)], held.at[pl.ds(i * rows, rows)], pooled.at[pl.ds(i * rows, rows)])
-        for i in range(PIECES)
-    ] + [(gw_in, held_gw, gw)]
-    loads = [pltpu.make_async_copy(src, mid, sems.at[0, i]) for i, (src, mid, _) in enumerate(pieces)]
-    stores = [pltpu.make_async_copy(mid, dst, sems.at[1, i]) for i, (_, mid, dst) in enumerate(pieces)]
+    pieces = [(small_in, small, None), (gw_in, held_gw, gw)]
+    for i in range(PIECES):
+        span = pl.ds(i * rows, rows)
+        pieces.append((pooled_in.at[span], held.at[span], pooled.at[span]))
+    loads = [
+        pltpu.make_async_copy(src, mid, load_sem.at[i]) for i, (src, mid, _) in enumerate(pieces)
+    ]
     for load in loads:
         load.start()
-    for load, store in zip(loads, stores):
+    stores = []
+
+    def store(src, dst):
+        copy = pltpu.make_async_copy(src, dst, store_sem.at[len(stores)])
+        stores.append(copy)
+        copy.start()
+
+    for load, (_, mid, dst) in zip(loads[1:], pieces[1:]):
         load.wait()
-        store.start()
-    gpb[...] = small[part_h : part_h + 1, :part1]
+        store(mid, dst)
+    loads[0].wait()
+    out_pb[...] = small[part_h : part_h + 1, :part1]
     low, high = small[:part_h, :64], small[:part_h, 64:]
     channels = jnp.concatenate([low, high, jnp.zeros((128 - part0, 64), F32)], axis=0)
     turned[...] = jnp.concatenate([channels, channels], axis=1).T
     for letter in range(4):
-        gew[:, letter, :] = turned[16 * letter : 16 * letter + kernel_width, :part0]
-    geb[...] = turned[15:16, :part0]
-    ggain[...] = turned[31:32, :part0]
-    for store in stores:
-        store.wait()
+        out_ew[:, letter, :] = turned[16 * letter : 16 * letter + kernel_width, :part0]
+    out_eb[...] = turned[15:16, :part0]
+    out_gain[...] = turned[31:32, :part0]
+    store(out_pb, gpb)
+    store(out_ew, gew)
+    store(out_eb, geb)
+    store(out_gain, ggain)
+    for copy in stores:
+        copy.wait()
 
 
 def shape(dims, kind):
@@ -390,7 +413,7 @@
         ((16, length), jnp.int32),
         ((length, 128), F32),
         ((2, half, 64), BF16),
-        ((2, 128, d0), F32),
+        ((2, big, d0), F32),
         ((2, half, d0), F32),
         ((2, half, d0), F32),
         ((2, half, 128), F32),
@@ -422,7 +445,7 @@
         in_specs=[hbm] * 7,
         out_specs=(hbm, vmem, vmem),
         scratch_shapes=[pltpu.VMEM(dims, kind) for dims, kind in scratch]
-        + [dma((n,)) for n in (72, 2, dp)]
+        + [dma((n,)) for n in (96, 2, dp)]
         + [dma((dp, 2)), dma((2,)), dma((2, 4)), dma((4,)), dma((2,)), dma((dp,)), dma((seq,)), dma((9,))],
         compiler_params=pltpu.CompilerParams(
             collective_id=0, has_side_effects=True, vmem_limit_bytes=60 * 2**20
@@ -442,13 +465,19 @@
             shape((part0, d1), F32),
             shape((1, part1), F32),
         ),
-        in_specs=[pl.BlockSpec(memory_space=pl.ANY), pl.BlockSpec(memory_space=pl.ANY), vmem],
-        out_specs=(hbm, vmem, vmem, vmem, hbm, vmem),
+        in_specs=[hbm] * 3,
+        out_specs=(hbm,) * 6,
         scratch_shapes=[
             pltpu.VMEM((128, 128), F32),
             pltpu.VMEM((half, d1), BF16),
             pltpu.VMEM((part0, d1), F32),
-            dma((2, PIECES + 1)),
+            pltpu.VMEM((part_h + 16, 128), F32),
+            pltpu.VMEM(embed_weight.shape, F32),
+            pltpu.VMEM((1, part0), F32),
+            pltpu.VMEM((1, part0), F32),
+            pltpu.VMEM((1, part1), F32),
+            dma((PIECES + 2,)),
+            dma((PIECES + 5,)),
         ],
         compiler_params=pltpu.CompilerParams(vmem_limit_bytes=60 * 2**20),
         name="finish_step",

time: 50 us -> 48.1 us (0.962)
  Pallas kernels: 49.2 us -> 47.2 us
    pallas_call x1, Pallas kernels: 3.63 us -> 2.38 us  [fused(): pl.pallas_call(functools.partial(finish_kernel, kernel_width), out_shape=...]
    pallas_call x1, Pallas kernels: 45.5 us -> 44.9 us  [fused(): pl.pallas_call(functools.partial(fused_kernel, kernel_width), out_shape=(...]
where the time goes in v5:
time: 48.1 us; the launch traced here: 47.9 us
  Pallas kernels  47.2 us (98%)
  between operations  0.64 us (1%)
    pallas_call x1, Pallas kernels, fused(): pl.pallas_call(functools.partial(fused_kernel, kernel_width), out_shape=(...  44.9 us
    pallas_call x1, Pallas kernels, fused(): pl.pallas_call(functools.partial(finish_kernel, kernel_width), out_shape=...  2.38 us

profile of v5, /device:TPU:0, one launch (start us, length us, event | category | flops | bytes accessed | tf_op | source)
XLA Modules:
  0.0 47.9 jit_solution(12595412582369818682)
XLA Ops:
  0.6 44.9 %fused_step.1 = (bf16[768,896]{1,0:T(8,128)(2,1)}, f32[96,896]{1,0:T(8,128)}, f32[64,128]{1,0:T(8,128)}) custom-call(s32[1,1536]{1,0:T(1,128)} %bases_hbm.1, bf16[15,4,96]{2,1,0:T(4,128)(2,1)} %ew_hbm.1, bf16[1,96]{1,0:T(2,128)(2,1)} %bitcast.9, bf16[1,96]{1,0:T(2,128)(2,1)} %bitcast.10, bf16[96,896]{1,0:T(8,128)(2,1)} %w_hbm.1, bf16[1,112]{1,0:T(2,128)(2,1)} %bitcast.11, ...), custom_call_target="tpu_custom_call" | custom-call | tf_op jit(solution)/shard_map/fused_step/pallas_call | solution.py:440
  45.5 2.4 %finish_step.1 = (bf16[768,896]{1,0:T(8,128)(2,1)}, f32[15,4,96]{2,1,0:T(4,128)}, f32[1,96]{1,0:T(1,128)}, f32[1,96]{1,0:T(1,128)}, f32[96,896]{1,0:T(8,128)}, /*index=5*/f32[1,112]{1,0:T(1,128)}) custom-call(bf16[768,896]{1,0:T(8,128)(2,1)} %get-tuple-element.15.pooled_in, f32[96,896]{1,0:T(8,128)} %get-tuple-element.16.gw_in, ...), custom_call_target="tpu_custom_call" | custom-call | tf_op jit(solution)/shard_map/finish_step/pallas_call | solution.py:458

commit v6 on v5

--- a/solution.py
+++ b/solution.py
@@ -39,16 +39,23 @@
         feat_ref[parity] = wide_ref[pl.ds(parity, half, stride=2), :][:, :64].astype(BF16)
 
 
+def wide(lanes, width):
+    return jnp.concatenate([lanes] * (width // 128), axis=1)
+
+
 def forward_chunk(start, size, feat_ref, weight, gain, emb_ref, scaled_ref, slope_ref, inv_ref, pact_ref):
+    width = gain.shape[1]
     for parity in range(2):
-        emb_ref[parity] = dot(feat_ref[parity, pl.ds(start, size), :], weight, NT)
+        emb = dot(feat_ref[parity, start : start + size, :], weight, NT)
+        emb = emb.astype(BF16).astype(F32)
+        emb_ref[parity] = emb
+        inverse = lax.rsqrt(jnp.sum(emb * emb, axis=1, keepdims=True) * (1.0 / width) + 1e-6)
+        inv_ref[parity, start : start + size, :] = jnp.broadcast_to(inverse, (size, 128))
     for r in range(0, size, STEP):
-        rows = pl.ds(start + r, STEP)
+        rows = slice(start + r, start + r + STEP)
         total = None
         for parity in range(2):
-            emb = emb_ref[parity, r : r + STEP, :].astype(BF16).astype(F32)
-            inverse = lax.rsqrt(jnp.mean(emb * emb, axis=1, keepdims=True) + 1e-6)
-            scaled = emb * inverse
+            scaled = emb_ref[parity, r : r + STEP, :] * wide(inv_ref[parity, rows, :], width)
             x = scaled * gain
             sq = x * x
             t = 0.5 + 0.5 * jnp.tanh(x * (ROOT + (ROOT * CUBIC) * sq))
@@ -56,12 +63,13 @@
             slope = t + act * (1.0 - t) * (2.0 * ROOT + (6.0 * ROOT * CUBIC) * sq)
             scaled_ref[parity, rows, :] = scaled
             slope_ref[parity, rows, :] = slope
-            inv_ref[parity, rows, :] = jnp.broadcast_to(inverse, (STEP, 128))
             total = act if total is None else total + act
         pact_ref[rows, :] = total.astype(BF16)
 
 
-def backward_chunk(start, size, cot_ref, w, gain, ga_ref, scaled_ref, slope_ref, inv_ref, ge_ref, acc_ref):
+def backward_chunk(
+    start, size, cot_ref, w, gain, ga_ref, mean_ref, scaled_ref, slope_ref, inv_ref, ge_ref, acc_ref
+):
     ga_ref[...] = dot(cot_ref[start : start + size, :], w, NT)
     width = ga_ref.shape[1]
     acc = acc_ref[...]
@@ -69,22 +77,26 @@
         rows = slice(start + r, start + r + STEP)
         ga = ga_ref[r : r + STEP, :]
         for parity in range(2):
-            scaled = scaled_ref[parity, rows, :]
-            inverse = inv_ref[parity, rows, 0:1]
-            u = ga * slope_ref[parity, rows, :]
-            q = u * scaled
+            q = ga * slope_ref[parity, rows, :] * scaled_ref[parity, rows, :]
             acc = acc + (q[:8] + q[8:])
             mean = jnp.sum(q * gain, axis=1, keepdims=True) * (1.0 / width)
-            ge = inverse * (u * gain - scaled * mean)
+            mean_ref[parity, r : r + STEP, :] = jnp.broadcast_to(mean, (STEP, 128))
+    acc_ref[...] = acc
+    for r in range(0, size, STEP):
+        rows = slice(start + r, start + r + STEP)
+        back = ga_ref[r : r + STEP, :] * gain
+        for parity in range(2):
+            mean = wide(mean_ref[parity, r : r + STEP, :], width)
+            inverse = wide(inv_ref[parity, rows, :], width)
+            ge = inverse * (back * slope_ref[parity, rows, :] - scaled_ref[parity, rows, :] * mean)
             ge_ref[parity, rows, :] = ge.astype(BF16)
-    acc_ref[...] = acc
 
 
 def fused_kernel(
     kernel_width,
     bases_hbm, ew_hbm, eb_hbm, gain_hbm, w_hbm, pb_hbm, cot_hbm,
     pooled_hbm, gw_ref, small_out,
-    pooled, bases, ew, eb, gain_in, pb, halo, stack, wide, feat, emb, scaled, slope, inv, pact, ge, ga, acc,
+    pooled, bases, ew, eb, gain_in, pb, halo, stack, turned_feat, feat, emb, scaled, slope, inv, pact, ge, ga, mean, acc,
     rows_in, pack, packs, wbuf, cot, gwb, s1buf, p1, s2buf, sum2, s3buf, fin, small, sbuf, tbuf,
     send_sem, halo_recv, pack_recv, w_recv, s1_recv, s2_recv, s3_recv, fin_recv,
     small_recv, t_recv, local_sem,
@@ -195,7 +207,7 @@
             halo[side : side + 1, :] = halo[side : side + 1, :] + 1
 
 
-    build_features(bases, halo, stack, wide, feat, kernel_width)
+    build_features(bases, halo, stack, turned_feat, feat, kernel_width)
     for j in range(1, dp):
         arrive(packs.at[(me + j) % dp], pack_recv.at[(me + j) % dp])
     shard_out((3, 2))
@@ -204,14 +216,10 @@
     )
     lanes = lax.broadcasted_iota(jnp.int32, (16, 64), 1)
     gain = dot(jnp.where(lanes == 31, 1.0, 0.0).astype(BF16), weight, NT)[0:1]
-    size = 256
-    chunks = half // size
-
-    def forward(first, last):
-        @pl.loop(first, last)
-        def _(i):
-            start = pl.multiple_of(i * size, size)
-            forward_chunk(start, size, feat, weight, gain, emb, scaled, slope, inv, pact)
+    size = half // 3
+
+    def forward(i):
+        forward_chunk(i * size, size, feat, weight, gain, emb.at[i % 2], scaled, slope, inv, pact)
 
     def relay(distances):
         for zz in range(4):
@@ -223,12 +231,13 @@
                 send(slot, slot, sem, 2 * z + y2, pos, there)
                 send(slot, slot, sem, me, mate, there)
 
-    forward(0, chunks // 3)
+    forward(0)
     relay((1,))
     d = 2 * z + y2
     arrive(wbuf.at[d, c], w_recv.at[d, c])
     send(wbuf.at[d, c], wbuf.at[d, c], w_recv.at[d, c], me, mate)
-    forward(chunks // 3, chunks)
+    forward(1)
+    forward(2)
 
     loads[7].wait()
     block = d0 // 2
@@ -274,7 +283,7 @@
 
     def backward(i):
         w = wbuf[...].reshape(d0, d1)
-        backward_chunk(i * big, big, cot, w, gain, ga.at[i % 2], scaled, slope, inv, ge, acc)
+        backward_chunk(i * big, big, cot, w, gain, ga.at[i % 2], mean.at[i % 2], scaled, slope, inv, ge, acc)
 
     def plane_sum(k):
         total = p1[k, rank].astype(F32)
@@ -413,13 +422,14 @@
         ((16, length), jnp.int32),
         ((length, 128), F32),
         ((2, half, 64), BF16),
-        ((2, big, d0), F32),
+        ((2, 2, big, d0), F32),
         ((2, half, d0), F32),
         ((2, half, d0), F32),
         ((2, half, 128), F32),
         ((half, d0), BF16),
         ((2, half, d0), BF16),
         ((2, big, d0), F32),
+        ((2, 2, big, 128), F32),
         ((8, d0), F32),
         ((128, 128), F32),
         ((part_h + 16, 128), BF16),

time: 48.1 us -> 48.9 us (1.017)
  Pallas kernels: 47.2 us -> 47.7 us
where the time goes in v6:
time: 48.9 us; the launch traced here: 48.3 us
  Pallas kernels  47.7 us (98%)
  between operations  0.64 us (1%)
    pallas_call x1, Pallas kernels, fused(): pl.pallas_call(functools.partial(fused_kernel, kernel_width), out_shape=(...  45.3 us
    pallas_call x1, Pallas kernels, fused(): pl.pallas_call(functools.partial(finish_kernel, kernel_width), out_shape=...  2.38 us

profile of v6, /device:TPU:0, one launch (start us, length us, event | category | flops | bytes accessed | tf_op | source)
XLA Modules:
  0.0 48.3 jit_solution(16332385916392836520)
XLA Ops:
  0.6 45.3 %fused_step.1 = (bf16[768,896]{1,0:T(8,128)(2,1)}, f32[96,896]{1,0:T(8,128)}, f32[64,128]{1,0:T(8,128)}) custom-call(s32[1,1536]{1,0:T(1,128)} %bases_hbm.1, bf16[15,4,96]{2,1,0:T(4,128)(2,1)} %ew_hbm.1, bf16[1,96]{1,0:T(2,128)(2,1)} %bitcast.9, bf16[1,96]{1,0:T(2,128)(2,1)} %bitcast.10, bf16[96,896]{1,0:T(8,128)(2,1)} %w_hbm.1, bf16[1,112]{1,0:T(2,128)(2,1)} %bitcast.11, ...), custom_call_target="tpu_custom_call" | custom-call | tf_op jit(solution)/shard_map/fused_step/pallas_call | solution.py:450
  46.0 2.4 %finish_step.1 = (bf16[768,896]{1,0:T(8,128)(2,1)}, f32[15,4,96]{2,1,0:T(4,128)}, f32[1,96]{1,0:T(1,128)}, f32[1,96]{1,0:T(1,128)}, f32[96,896]{1,0:T(8,128)}, /*index=5*/f32[1,112]{1,0:T(1,128)}) custom-call(bf16[768,896]{1,0:T(8,128)(2,1)} %get-tuple-element.15.pooled_in, f32[96,896]{1,0:T(8,128)} %get-tuple-element.16.gw_in, ...), custom_call_target="tpu_custom_call" | custom-call | tf_op jit(solution)/shard_map/finish_step/pallas_call | solution.py:468

commit v7 on v6

--- a/solution.py
+++ b/solution.py
@@ -249,17 +249,15 @@
             relay((2, 3))
 
     rank = 2 * x + y
-    others = (
-        (2 * x2 + y2, 2 * z + y2, across),
-        (2 * x + y2, 2 * z + y2, pos),
-        (2 * x2 + y, me, across),
-    )
     for b in range(2):
         arrive(s1buf.at[b], s1_recv.at[b])
         for k in range(4):
             p1[b, k] = (gwb[4 * b + k, c].astype(F32) + s1buf[b, k].astype(F32)).astype(BF16)
-        for piece, to_dp, to_seq in others:
-            send(p1.at[b, piece], s2buf.at[b, rank], s2_recv.at[b, rank], to_dp, to_seq)
+        if b == 0:
+            send(p1.at[0, pl.ds(2 * x2, 2)], s2buf.at[0, 0:2], s2_recv.at[0, 0], me, across)
+        else:
+            for xx in range(2):
+                send(p1.at[1, 2 * xx + y2], s2buf.at[1, xx], s2_recv.at[1, xx], 2 * z + y2, pos)
 
     for zz in range(4):
         d = 2 * zz + y2
@@ -285,16 +283,28 @@
         w = wbuf[...].reshape(d0, d1)
         backward_chunk(i * big, big, cot, w, gain, ga.at[i % 2], mean.at[i % 2], scaled, slope, inv, ge, acc)
 
+    def add(k, piece, arrived):
+        p1[k, piece] = (p1[k, piece].astype(F32) + s2buf[k, arrived].astype(F32)).astype(BF16)
+
+    def pair_sums():
+        arrive(s2buf.at[0, 0:2], s2_recv.at[0, 0])
+        for yy in range(2):
+            add(0, 2 * x + yy, yy)
+        send(p1.at[0, 2 * x + y2], s2buf.at[0, 2], s2_recv.at[0, 2], 2 * z + y2, pos)
+        for xx in range(2):
+            arrive(s2buf.at[1, xx], s2_recv.at[1, xx])
+            add(1, 2 * xx + y, xx)
+        send(p1.at[1, 2 * x2 + y], s2buf.at[1, 2], s2_recv.at[1, 2], me, across)
+
     def plane_sum(k):
-        total = p1[k, rank].astype(F32)
-        for piece, _, _ in others:
-            arrive(s2buf.at[k, piece], s2_recv.at[k, piece])
-            total = total + s2buf[k, piece].astype(F32)
+        arrive(s2buf.at[k, 2], s2_recv.at[k, 2])
+        total = p1[k, rank].astype(F32) + s2buf[k, 2].astype(F32)
         sum2[k] = total.astype(BF16)
         zt = x + 2 * k
         send(sum2.at[k], s3buf.at[z], s3_recv.at[z], 2 * zt + y, pos, zt != z)
 
     backward(0)
+    pair_sums()
     backward(1)
     plane_sum(0)
     backward(2)

time: 48.9 us -> 49.6 us (1.014)
  Pallas kernels: 47.7 us -> 48.4 us
    pallas_call x1, Pallas kernels: 45.3 us -> 46 us  [fused(): pl.pallas_call(functools.partial(fused_kernel, kernel_width), out_shape=(...]
where the time goes in v7:
time: 49.6 us; the launch traced here: 49.1 us
  Pallas kernels  48.4 us (98%)
  between operations  0.64 us (1%)
    pallas_call x1, Pallas kernels, fused(): pl.pallas_call(functools.partial(fused_kernel, kernel_width), out_shape=(...  46 us
    pallas_call x1, Pallas kernels, fused(): pl.pallas_call(functools.partial(finish_kernel, kernel_width), out_shape=...  2.38 us

profile of v7, /device:TPU:0, one launch (start us, length us, event | category | flops | bytes accessed | tf_op | source)
XLA Modules:
  0.0 49.1 jit_solution(7554442841891599685)
XLA Ops:
  0.6 46.0 %fused_step.1 = (bf16[768,896]{1,0:T(8,128)(2,1)}, f32[96,896]{1,0:T(8,128)}, f32[64,128]{1,0:T(8,128)}) custom-call(s32[1,1536]{1,0:T(1,128)} %bases_hbm.1, bf16[15,4,96]{2,1,0:T(4,128)(2,1)} %ew_hbm.1, bf16[1,96]{1,0:T(2,128)(2,1)} %bitcast.9, bf16[1,96]{1,0:T(2,128)(2,1)} %bitcast.10, bf16[96,896]{1,0:T(8,128)(2,1)} %w_hbm.1, bf16[1,112]{1,0:T(2,128)(2,1)} %bitcast.11, ...), custom_call_target="tpu_custom_call" | custom-call | tf_op jit(solution)/shard_map/fused_step/pallas_call | solution.py:460
  46.7 2.4 %finish_step.1 = (bf16[768,896]{1,0:T(8,128)(2,1)}, f32[15,4,96]{2,1,0:T(4,128)}, f32[1,96]{1,0:T(1,128)}, f32[1,96]{1,0:T(1,128)}, f32[96,896]{1,0:T(8,128)}, /*index=5*/f32[1,112]{1,0:T(1,128)}) custom-call(bf16[768,896]{1,0:T(8,128)(2,1)} %get-tuple-element.15.pooled_in, f32[96,896]{1,0:T(8,128)} %get-tuple-element.16.gw_in, ...), custom_call_target="tpu_custom_call" | custom-call | tf_op jit(solution)/shard_map/finish_step/pallas_call | solution.py:478
